TPU v7x, 32 devices: a whole 2x2x4 slice. The times are simulated.
32 devices in a mesh: section: 2 (over core), dp: 2 (over x), ctx: 2 (over y), tp: 4 (over z).
Axes of the slice: x: 2, y: 2, z: 4, core: 2. Of those that a mesh axis runs over, the one named last changes fastest.
Arguments:
- section_in: bfloat16 [2, 4, 1024, 1536], P(None, 'dp', 'ctx'), may hold values from -6 to 6
- segments: int32 [2, 4, 1024], P(None, 'dp', 'ctx'), may hold values from 0 to 5, as said below
- positions: int32 [2, 4, 1024], P(None, 'dp', 'ctx'), may hold values from 0 to 3070, as said below
- query_weight: bfloat16 [2, 1536, 1536], P('section', ('dp', 'ctx'), 'tp'), may hold values from -0.15625 to 0.15625
- kv_weight: bfloat16 [2, 2, 1536, 256], P('section', None, ('dp', 'ctx')), may hold values from -0.15625 to 0.15625
- output_weight: bfloat16 [2, 1536, 1536], P('section', 'tp', ('dp', 'ctx')), may hold values from -0.625 to 0.625
- gate_up: bfloat16 [2, 2, 1536, 8960], P('section', None, ('dp', 'ctx'), 'tp'), may hold values from -0.15625 to 0.15625
- down_weight: bfloat16 [2, 8960, 1536], P('section', 'tp', ('dp', 'ctx')), may hold values from -0.125 to 0.125
- norm_gains: bfloat16 [2, 2, 1536], P('section', None, ('dp', 'ctx')), may hold values from 0.099609375 to 1.8984375
- query_bias: bfloat16 [2, 12, 128], P('section', 'tp', ('dp', 'ctx')), may hold values from -3 to 3
- kv_bias: bfloat16 [2, 2, 2, 128], P('section', None, None, ('dp', 'ctx')), may hold values from -3 to 3
- out_grad: bfloat16 [2, 4, 1024, 1536], P(None, 'dp', 'ctx'), may hold values from -6 to 6
Outputs:
- section_out: bfloat16 [2, 2, 4, 1024, 1536], P('section', None, 'dp', 'ctx')
- input_grad: bfloat16 [2, 2, 4, 1024, 1536], P('section', None, 'dp', 'ctx')
- query_weight_grad: float32 [2, 1536, 1536], P('section', ('dp', 'ctx'), 'tp')
- kv_weight_grad: float32 [2, 2, 1536, 256], P('section', None, ('dp', 'ctx'))
- output_weight_grad: float32 [2, 1536, 1536], P('section', 'tp', ('dp', 'ctx'))
- gate_up_grad: float32 [2, 2, 1536, 8960], P('section', None, ('dp', 'ctx'), 'tp')
- down_weight_grad: float32 [2, 8960, 1536], P('section', 'tp', ('dp', 'ctx'))
- norm_gains_grad: float32 [2, 2, 1536], P('section', None, ('dp', 'ctx'))
- query_bias_grad: float32 [2, 12, 128], P('section', 'tp', ('dp', 'ctx'))
- kv_bias_grad: float32 [2, 2, 2, 128], P('section', None, None, ('dp', 'ctx'))
Inputs may be any that keep to these rules, and one draw needn't show every extreme that they name: `segments`: in each sequence the numbers start at 0 and rise by one where a document begins; documents hold 200 to 900 tokens, except the last one, which the sequence's end cuts. In each micro-batch, on each index of dp, one of the 2 sequences is a single document, and another is packed with as many documents as fit, so that its last number is the promised most. `positions`: A token's position is its place within its document plus an offset below 2048 drawn for each document.
All inputs are finite; a program needn't handle non-finite values.
Results may differ from a plain program's by a relative error of at most 0.03.
Values may be sent and summed in bfloat16 or wider, within the bound.
A program may use at most 448 MiB of HBM per device.

v0:
```python
import functools

import jax
import jax.numpy as jnp
from jax import lax
from jax.experimental import pallas as pl
from jax.experimental.pallas import tpu as pltpu
from jax.sharding import PartitionSpec as P

HEADS = 12
KV_HEADS = 2
HEAD = 128

EPS = 1e-06
ROPE_BASE = 1000000.0
NEG = -1e30
SCALE = HEAD ** (-0.5)
TILE = 768
VMEM_LIMIT = 60 << 20
MESH = pl.DeviceIdType.MESH

F32 = jnp.float32
BF16 = jnp.bfloat16


def dot(form, left, right):
    return jnp.einsum(form, left, right, preferred_element_type=F32)


def swap(value):
    return lax.ppermute(value, "section", [(0, 1), (1, 0)])


class Chain:
    def __init__(self, part, total, from_end, from_peer, sems):
        self.part, self.total = part, total
        self.from_end, self.from_peer = from_end, from_peer
        self.sems = sems
        self.chunks = sems.shape[1]
        self.rows = part.shape[0] // self.chunks
        self.is_middle, self.inner, self.outer = line_places()

    def at(self, ref, c):
        return ref.at[pl.ds(pl.multiple_of(c * self.rows, self.rows), self.rows)]

    def copy(self, source, target, c, step, place):
        return pltpu.make_async_remote_copy(
            src_ref=self.at(source, c),
            dst_ref=self.at(target, c),
            send_sem=self.sems.at[2 * step, c],
            recv_sem=self.sems.at[2 * step + 1, c],
            device_id={"tp": place},
            device_id_type=MESH,
        )

    def inward(self, c):
        return self.copy(self.part, self.from_end, c, 0, self.inner)

    def across(self, c):
        return self.copy(self.total, self.from_peer, c, 1, self.inner)

    def outward(self, c):
        return self.copy(self.total, self.total, c, 2, self.outer)

    def start(self):
        @pl.when(jnp.logical_not(self.is_middle))
        def _():
            @pl.loop(0, self.chunks)
            def _(c):
                self.inward(c).start()

    def join(self, c):
        self.inward(c).wait_recv()
        self.at(self.total, c)[...] = self.at(self.part, c)[...] + self.at(self.from_end, c)[...]
        self.across(c).start()

    def close(self, c):
        self.across(c).wait()
        self.at(self.total, c)[...] = self.at(self.total, c)[...] + self.at(self.from_peer, c)[...]
        self.outward(c).start()

    def step(self, c):
        @pl.when(self.is_middle & (c < self.chunks))
        def _():
            self.join(c)

            @pl.when(c > 0)
            def _():
                self.close(c - 1)

    def drain(self, done):
        @pl.when(self.is_middle)
        def _():
            if done < self.chunks:

                @pl.loop(done, self.chunks)
                def _(c):
                    self.step(c)

            self.close(self.chunks - 1)

        @pl.when(jnp.logical_not(self.is_middle))
        def _():
            @pl.loop(0, self.chunks)
            def _(c):
                self.outward(c).wait_recv()

    def settle(self):
        @pl.when(self.is_middle)
        def _():
            @pl.loop(0, self.chunks)
            def _(c):
                self.outward(c).wait_send()

        @pl.when(jnp.logical_not(self.is_middle))
        def _():
            @pl.loop(0, self.chunks)
            def _(c):
                self.inward(c).wait_send()


def line_places():
    place = lax.axis_index("tp")
    is_middle = (place == 1) | (place == 2)
    return is_middle, jnp.where(place < 2, place + 1, place - 1), jnp.where(place < 2, place - 1, place + 1)


def greet(ctx_count=1, cores=0):
    is_middle, inner, outer = line_places()
    me = lax.axis_index("ctx")
    barrier = pltpu.get_barrier_semaphore()
    for step in range(1, ctx_count):
        pl.semaphore_signal(barrier, inc=1, device_id={"ctx": lax.rem(me + step, ctx_count)}, device_id_type=MESH)
    if cores:
        peer = 1 - lax.axis_index("section")
        pl.semaphore_signal(barrier, inc=1, device_id={"section": peer}, device_id_type=MESH)
    pl.semaphore_signal(barrier, inc=1, device_id={"tp": inner}, device_id_type=MESH)

    @pl.when(is_middle)
    def _():
        pl.semaphore_signal(barrier, inc=1, device_id={"tp": outer}, device_id_type=MESH)
        pl.semaphore_wait(barrier, 1 + ctx_count + cores)

    @pl.when(jnp.logical_not(is_middle))
    def _():
        pl.semaphore_wait(barrier, ctx_count + cores)


def ab(ref):
    rows = ref.shape[0] // 2
    return ref.at[pl.ds(0, rows)], ref.at[pl.ds(rows, rows)]


def chain_scratch(shape):
    return [pltpu.VMEM(shape, BF16)] * 2 + [pltpu.SemaphoreType.DMA((6, min(8, shape[0] // 16)))]


CHAIN_REFS = 3
VMEM = pl.BlockSpec(memory_space=pltpu.VMEM)
ANY = pl.BlockSpec(memory_space=pl.ANY)


def params(collective_id):
    return pltpu.CompilerParams(collective_id=collective_id, has_side_effects=True, vmem_limit_bytes=VMEM_LIMIT)


def cost():
    return pl.CostEstimate(flops=1 << 20, bytes_accessed=1 << 20, transcendentals=0)


class Taker:
    def __init__(self, refs):
        self.refs = list(refs)

    def __call__(self, count):
        taken, self.refs = self.refs[:count], self.refs[count:]
        return taken


def ticker(chain, taken):
    return (lambda c: None) if chain is None else (lambda c: chain.step(c + taken))


def mm(left, right):
    return jnp.dot(left, right, preferred_element_type=F32)


def mm_t(left, right):
    return lax.dot_general(left, right, (((1,), (1,)), ((), ())), preferred_element_type=F32)


def mm_0(left, right):
    return lax.dot_general(left, right, (((0,), (0,)), ((), ())), preferred_element_type=F32)


def tile_at(ref, j, size=TILE):
    return ref.at[:, pl.ds(pl.multiple_of(j * size, size), size)]


def rows_at(ref, j, size=TILE):
    return ref.at[pl.ds(pl.multiple_of(j * size, size), size)]


def by_rows(rows, body, block=64):
    @pl.loop(0, rows // block)
    def _(i):
        body(pl.ds(pl.multiple_of(i * block, block), block))


def send_either(first, source, one, two, sem, start):
    @pl.when(first)
    def _():
        copy = pltpu.make_async_copy(source, one, sem)
        copy.start() if start else copy.wait()

    @pl.when(jnp.logical_not(first))
    def _():
        copy = pltpu.make_async_copy(source, two, sem)
        copy.start() if start else copy.wait()


def norm_factor(values):
    return lax.rsqrt(jnp.mean(values * values, axis=-1, keepdims=True) + EPS)


def normalize_rows(source, gain, target):
    def body(rows):
        values = source(rows)
        target[rows] = (values * norm_factor(values) * gain[...]).astype(BF16)

    by_rows(target.shape[0], body)


def norm_back_rows(upstream, grad_in, source, gain, gain_grad, target):
    def body(rows):
        values = source(rows)
        factor = norm_factor(values)
        unit = values * factor
        grad = grad_in[rows].astype(F32)
        per_row = grad * unit
        mean = jnp.mean(per_row * gain[...], axis=-1, keepdims=True)
        target[rows] = (upstream[rows].astype(F32) + factor * (grad * gain[...] - unit * mean)).astype(BF16)
        gain_grad[...] += jnp.sum(per_row.reshape(-1, 8, per_row.shape[1]), axis=0)

    by_rows(target.shape[0], body)


class FfnWeights:
    def __init__(self, sources, targets, sems, down_sems, by_columns):
        self.own, self.down_own = sources
        self.gate, self.up, self.down = targets
        self.sems, self.down_sems = sems, down_sems
        self.sec = lax.axis_index("section")
        self.first = self.sec == 0
        self.by_columns = by_columns
        self.wide = tile_at if by_columns else rows_at
        self.tiles, self.outs = self.gate.shape[1] // TILE, self.gate.shape[0] // TILE
        self.wide_count, self.deep_count = (self.tiles, self.outs) if by_columns else (self.outs, self.tiles)

    def here(self, j, target):
        return pltpu.make_async_copy(self.wide(self.own, j), self.wide(target, j), self.sems.at[0, j])

    def there(self, j, target):
        return pltpu.make_async_remote_copy(
            src_ref=self.wide(self.own, j),
            dst_ref=self.wide(target, j),
            send_sem=self.sems.at[1, j],
            recv_sem=self.sems.at[2, j],
            device_id={"section": 1 - self.sec},
            device_id_type=MESH,
        )

    def on_own(self, action):
        @pl.when(self.first)
        def _():
            action(self.gate, self.up)

        @pl.when(jnp.logical_not(self.first))
        def _():
            action(self.up, self.gate)

    def wait_gate(self, j):
        @pl.when(self.first)
        def _():
            self.here(j, self.gate).wait()

        @pl.when(jnp.logical_not(self.first))
        def _():
            self.there(j, self.gate).wait_recv()

    def wait_up(self, j):
        @pl.when(self.first)
        def _():
            self.there(j, self.up).wait_recv()

        @pl.when(jnp.logical_not(self.first))
        def _():
            self.here(j, self.up).wait()

    def down_parts(self, j):
        shards, half = self.down_own.shape[0], self.down_own.shape[1]
        per_tile = shards if not self.by_columns else shards // self.outs
        for i in range(per_tile):
            if self.by_columns:
                shard = j * per_tile + i
                source, columns = self.down_own.at[shard], slice(None)
            else:
                shard, columns = i, pl.ds(pl.multiple_of(j * TILE, TILE), TILE)
                source = self.down_own.at[shard, :, columns]

            def place(sec, shard=shard, columns=columns):
                return self.down.at[pl.ds(pl.multiple_of((2 * shard + sec) * half, 16), half), columns]

            yield source, place(self.sec), place(1 - self.sec), i

    def down_here(self, source, place, i, j):
        return pltpu.make_async_copy(source, place, self.down_sems.at[0, j, i])

    def down_there(self, source, place, i, j):
        return pltpu.make_async_remote_copy(
            src_ref=source,
            dst_ref=place,
            send_sem=self.down_sems.at[1, j, i],
            recv_sem=self.down_sems.at[2, j, i],
            device_id={"section": 1 - self.sec},
            device_id_type=MESH,
        )

    def start_wide(self, local):
        def action(own, other):
            @pl.loop(0, self.wide_count)
            def _(j):
                (self.here if local else self.there)(j, own).start()

        self.on_own(action)

    def start_deep(self, local):
        @pl.loop(0, self.deep_count)
        def _(j):
            for source, mine, theirs, i in self.down_parts(j):
                (self.down_here if local else self.down_there)(source, mine, i, j).start()

    def wait_down(self, j):
        for source, mine, theirs, i in self.down_parts(j):
            self.down_here(source, mine, i, j).wait()
            self.down_there(source, theirs, i, j).wait_recv()

    def finish(self):
        def action(own, other):
            @pl.loop(0, self.wide_count)
            def _(j):
                self.there(j, own).wait_send()

        self.on_own(action)

        @pl.loop(0, self.deep_count)
        def _(j):
            for source, mine, theirs, i in self.down_parts(j):
                self.down_there(source, mine, i, j).wait_send()


def ffn_forward_stage(weights, normed, outs, held, one, two, out_sems, result, tick, wait):
    gate, up, inner = held

    @pl.loop(0, weights.tiles)
    def _(j):
        if wait:
            weights.wait_gate(j)
        one[...] = mm(normed[...], tile_at(weights.gate, j)[...])
        tick(2 * j)
        if wait:
            weights.wait_up(j)
        two[...] = mm(normed[...], tile_at(weights.up, j)[...])
        columns = pl.ds(pl.multiple_of(j * TILE, TILE), TILE)

        def body(rows):
            g, u = one[rows], two[rows]
            gate[rows, columns] = g.astype(BF16)
            up[rows, columns] = u.astype(BF16)
            inner[rows, columns] = (g * jax.nn.sigmoid(g) * u).astype(BF16)

        by_rows(one.shape[0], body)
        tick(2 * j + 1)
        for k in range(3):
            pltpu.make_async_copy(tile_at(held[k], j), tile_at(outs[k], j), out_sems.at[k, j]).start()

    @pl.loop(0, weights.outs)
    def _(n):
        if wait:
            weights.wait_down(n)
        tile_at(result, n)[...] = mm_t(inner[...], rows_at(weights.down, n)[...]).astype(BF16)
        tick(2 * weights.tiles + n)

    return 2 * weights.tiles + weights.outs


def wait_out(held, outs, out_sems):
    @pl.loop(0, held[0].shape[1] // TILE)
    def _(j):
        for k in range(len(held)):
            pltpu.make_async_copy(tile_at(held[k], j), tile_at(outs[k], j), out_sems.at[k, j]).wait()


def ffn_forward_kernel(lead, *refs):
    take = Taker(refs)
    layer, attn_a, last_b, gain = take(4)
    layer_a, layer_b = ab(layer)
    sources = take(2)
    (normed_a, normed_b), *outs = [ab(ref) for ref in take(4)]
    outs_a, outs_b = zip(*outs)
    result_b, total_a = take(2)
    attn_b = take(1)[0] if lead else last_b
    targets, held = take(3), take(3)
    one, two, result_a, w_sems, down_sems, out_sems = take(6)
    chain_a = Chain(result_a, total_a, *take(CHAIN_REFS))
    chain_b = Chain(last_b, attn_b, *take(CHAIN_REFS)) if lead else None
    weights = FfnWeights(sources, targets, w_sems, down_sems, True)
    weights.start_wide(True)
    weights.start_deep(True)
    greet(cores=1)
    if lead:
        chain_b.start()
    weights.start_wide(False)
    weights.start_deep(False)
    normalize_rows(lambda r: layer_a[r].astype(F32) + attn_a[r].astype(F32), gain, normed_a)
    if lead:
        chain_b.step(0)
    tick = ticker(chain_b, 1)
    done = ffn_forward_stage(weights, normed_a, outs_a, held, one, two, out_sems, result_a, tick, True)
    chain_a.start()
    if lead:
        chain_b.drain(1 + done)
        chain_a.step(0)
    normalize_rows(lambda r: layer_b[r].astype(F32) + attn_b[r].astype(F32), gain, normed_b)
    wait_out(held, outs_a, out_sems)
    if not lead:
        chain_a.step(0)
    tick = ticker(chain_a, 1)
    done = ffn_forward_stage(weights, normed_b, outs_b, held, one, two, out_sems, result_b, tick, False)
    chain_a.drain(1 + done)
    chain_a.settle()
    if lead:
        chain_b.settle()
    weights.finish()
    wait_out(held, outs_b, out_sems)


def down_sem_shape(weights, tiles):
    return pltpu.SemaphoreType.DMA((3, tiles, weights[1].shape[0]))


def ffn_forward(lead, layer_in, attn_a, last_b, gain, weights):
    rows, width = attn_a.shape
    ff = weights[0].shape[1]
    tiles = max(ff, width) // TILE
    narrow = jax.ShapeDtypeStruct((rows, width), BF16)
    both, wide = jax.ShapeDtypeStruct((2 * rows, width), BF16), jax.ShapeDtypeStruct((2 * rows, ff), BF16)
    return pl.pallas_call(
        functools.partial(ffn_forward_kernel, lead),
        out_shape=[both, wide, wide, wide] + [narrow] * (2 + lead),
        in_specs=[VMEM] * 4 + [ANY] * 2,
        out_specs=[VMEM] + [ANY] * 3 + [VMEM] * (2 + lead),
        scratch_shapes=[pltpu.VMEM((width, ff), BF16)] * 3
        + [pltpu.VMEM((rows, ff), BF16)] * 3
        + [pltpu.VMEM((rows, TILE), F32)] * 2
        + [pltpu.VMEM((rows, width), BF16)]
        + [pltpu.SemaphoreType.DMA((3, tiles)), down_sem_shape(weights, tiles), pltpu.SemaphoreType.DMA((3, tiles))]
        + chain_scratch((rows, width)) * (1 + lead),
        compiler_params=params(1 + lead),
        cost_estimate=cost(),
    )(layer_in, attn_a, last_b, gain, *weights)


def ffn_backward_stage(weights, grad, ins, outs, held, one, in_sems, out_sems, result, tick, wait):
    gate, up = held
    own_out, other_out = outs

    @pl.loop(0, weights.tiles)
    def _(j):
        if wait:
            weights.wait_down(j)
        one[...] = mm(grad[...], tile_at(weights.down, j)[...])
        tick(j)
        for k in range(2):
            pltpu.make_async_copy(tile_at(ins[k], j), tile_at(held[k], j), in_sems.at[k, j]).wait()
        columns = pl.ds(pl.multiple_of(j * TILE, TILE), TILE)

        def body(rows):
            g, u, d = gate[rows, columns].astype(F32), up[rows, columns].astype(F32), one[rows]
            sig = jax.nn.sigmoid(g)
            d = d * sig
            gate[rows, columns] = (d * u * (1.0 + g * (1.0 - sig))).astype(BF16)
            up[rows, columns] = (d * g).astype(BF16)

        by_rows(one.shape[0], body)

    def sending(start):
        @pl.loop(0, weights.tiles)
        def _(j):
            own, other = tile_at(own_out, j), tile_at(other_out, j)
            send_either(weights.first, tile_at(gate, j), own, other, out_sems.at[0, j], start)
            send_either(weights.first, tile_at(up, j), other, own, out_sems.at[1, j], start)

    sending(True)

    @pl.loop(0, weights.outs)
    def _(n):
        if wait:
            weights.wait_gate(n)
            weights.wait_up(n)
        one[...] = mm_t(gate[...], rows_at(weights.gate, n)[...])
        tick(weights.tiles + 2 * n)
        tile_at(result, n)[...] = (one[...] + mm_t(up[...], rows_at(weights.up, n)[...])).astype(BF16)
        tick(weights.tiles + 2 * n + 1)

    return weights.tiles + 2 * weights.outs, lambda: sending(False)


def ffn_backward_kernel(low, *refs):
    take = Taker(refs)
    grad, last_b = take(2)
    grad_a, grad_b = ab(grad)
    ins_a, ins_b = zip(*[ab(ref) for ref in take(2)])
    sources = take(2)
    if low:
        sum_a, layer, gain = take(3)
        layer_a, layer_b = ab(layer)
    outs_a, outs_b = zip(*[ab(ref) for ref in take(2)])
    result_b, total_a, total_b = take(3)
    if low:
        made, gain_grad = take(2)
        made_a, made_b = ab(made)
    targets, held = take(3), take(2)
    one, result_a, w_sems, down_sems, in_sems, out_sems = take(6)
    chain_a = Chain(result_a, total_a, *take(CHAIN_REFS))
    chain_b = Chain(last_b, total_b, *take(CHAIN_REFS))
    weights = FfnWeights(sources, targets, w_sems, down_sems, False)

    def fetch(ins):
        @pl.loop(0, weights.tiles)
        def _(j):
            for k in range(2):
                pltpu.make_async_copy(tile_at(ins[k], j), tile_at(held[k], j), in_sems.at[k, j]).start()

    weights.start_deep(True)
    fetch(ins_a)
    weights.start_wide(True)
    greet(cores=1)
    chain_b.start()
    weights.start_deep(False)
    weights.start_wide(False)
    if low:
        gain_grad[...] = jnp.zeros_like(gain_grad)
        norm_back_rows(grad_a, sum_a, lambda r: layer_a[r].astype(F32), gain, gain_grad, made_a)
        grad_a = made_a
    chain_b.step(0)
    done, sent_a = ffn_backward_stage(
        weights, grad_a, ins_a, outs_a, held, one, in_sems, out_sems, result_a, ticker(chain_b, 1), True
    )
    chain_a.start()
    sent_a()
    fetch(ins_b)
    chain_b.drain(1 + done)
    chain_a.step(0)
    if low:
        norm_back_rows(grad_b, total_b, lambda r: layer_b[r].astype(F32), gain, gain_grad, made_b)
        grad_b = made_b
    done, sent_b = ffn_backward_stage(
        weights, grad_b, ins_b, outs_b, held, one, in_sems, out_sems, result_b, ticker(chain_a, 1), False
    )
    chain_a.drain(1 + done)
    chain_a.settle()
    chain_b.settle()
    weights.finish()
    sent_b()


def ffn_backward(grad, gate, up, weights, last_b, below=None):
    rows, width = last_b.shape
    ff = weights[0].shape[1]
    tiles = max(ff, width) // TILE
    low = below is not None
    narrow = jax.ShapeDtypeStruct((rows, width), BF16)
    both, wide = jax.ShapeDtypeStruct((2 * rows, width), BF16), jax.ShapeDtypeStruct((2 * rows, ff), BF16)
    more = [both, jax.ShapeDtypeStruct((8, width), F32)] if low else []
    return pl.pallas_call(
        functools.partial(ffn_backward_kernel, low),
        out_shape=[wide] * 2 + [narrow] * 3 + more,
        in_specs=[VMEM] * 2 + [ANY] * 4 + [VMEM] * (3 if low else 0),
        out_specs=[ANY] * 2 + [VMEM] * (3 + len(more)),
        scratch_shapes=[pltpu.VMEM((width, ff), BF16)] * 3
        + [pltpu.VMEM((rows, ff), BF16)] * 2
        + [pltpu.VMEM((rows, TILE), F32)]
        + [pltpu.VMEM((rows, width), BF16)]
        + [pltpu.SemaphoreType.DMA((3, tiles)), down_sem_shape(weights, tiles)]
        + [pltpu.SemaphoreType.DMA((2, tiles))] * 2
        + chain_scratch((rows, width)) * 2,
        compiler_params=params(3 + low),
        cost_estimate=cost(),
    )(grad, last_b, gate, up, *weights, *(below or ()))


def last_kernel(part, sum_a, grad, layer, gain, made, gain_grad, total, *scratch):
    chain = Chain(part, total, *scratch)
    greet()
    chain.start()
    gain_grad[...] = jnp.zeros_like(gain_grad)
    grads, layers, mades = ab(grad), ab(layer), ab(made)
    chain.step(0)
    norm_back_rows(grads[0], sum_a, lambda r: layers[0][r].astype(F32), gain, gain_grad, mades[0])
    chain.drain(1)
    norm_back_rows(grads[1], total, lambda r: layers[1][r].astype(F32), gain, gain_grad, mades[1])
    chain.settle()


def last_grads(part, sum_a, grad, layer, gain):
    shape = part.shape
    return pl.pallas_call(
        last_kernel,
        out_shape=[jax.ShapeDtypeStruct(grad.shape, BF16), jax.ShapeDtypeStruct((8, shape[1]), F32)],
        in_specs=[VMEM] * 5,
        out_specs=[VMEM] * 2,
        scratch_shapes=[pltpu.VMEM(shape, BF16)] + chain_scratch(shape),
        compiler_params=params(0),
        cost_estimate=cost(),
    )(part, sum_a, grad, layer, gain)


def roped(values, cosine, sine):
    return values * cosine + pltpu.roll(values, HEAD // 2, 1) * sine


def unroped(grads, cosine, sine):
    return grads * cosine + pltpu.roll(grads * sine, HEAD // 2, 1)


def allowed_keys(seg_rows, seg_keys, i, block):
    rows, keys = seg_rows.shape[0], seg_keys.shape[1]
    first_row = lax.axis_index("ctx") * rows + i * block
    row_at = first_row + lax.broadcasted_iota(jnp.int32, (block, keys), 0)
    key_at = lax.broadcasted_iota(jnp.int32, (block, keys), 1)
    own = seg_rows[pl.ds(pl.multiple_of(i * block, block), block)]
    return (key_at <= row_at) & (own == seg_keys[...])


def attention_forward_stage(layer_in, gain, w_lin, w_out, bias, places, outs, result, kv_sems, tick):
    cosine, sine, seg_rows, seg_keys = places
    normed, query, kv, lse, attended = outs
    rows, q_cols = query.shape
    heads = q_cols // HEAD
    count = kv.shape[0] // rows
    me = lax.axis_index("ctx")
    block = min(256, rows)
    normalize_rows(lambda r: layer_in[r].astype(F32), gain, normed)
    tick(0)
    mine = kv.at[pl.ds(pl.multiple_of(me * rows, rows), rows)]
    lin = mm(normed[...], w_lin[:, q_cols:]) + bias[:, q_cols:]
    mine[:, :HEAD] = roped(lin[:, :HEAD], cosine[...], sine[...]).astype(BF16)
    mine[:, HEAD:] = lin[:, HEAD:].astype(BF16)

    def passing(offset):
        return pltpu.make_async_remote_copy(
            src_ref=mine,
            dst_ref=mine,
            send_sem=kv_sems.at[0, offset],
            recv_sem=kv_sems.at[1, offset],
            device_id={"ctx": lax.rem(me + offset, count)},
            device_id_type=MESH,
        )

    for offset in range(1, count):
        passing(offset).start()
    tick(1)
    lin = mm(normed[...], w_lin[:, :q_cols]) + bias[:, :q_cols]
    for h in range(heads):
        columns = slice(h * HEAD, (h + 1) * HEAD)
        query[:, columns] = roped(lin[:, columns], cosine[...], sine[...]).astype(BF16)
    for offset in range(1, count):
        passing(offset).wait_recv()

    @pl.loop(0, rows // block)
    def _(i):
        at = pl.ds(pl.multiple_of(i * block, block), block)
        allowed = allowed_keys(seg_rows, seg_keys, i, block)
        lane = lax.broadcasted_iota(jnp.int32, (block, HEAD), 1)
        logs = jnp.zeros((block, HEAD), F32)
        for h in range(heads):
            columns = slice(h * HEAD, (h + 1) * HEAD)
            scores = jnp.where(allowed, mm_t(query[at, columns], kv[:, :HEAD]) * SCALE, NEG)
            top = jnp.max(scores, axis=-1, keepdims=True)
            probs = jnp.exp(scores - top)
            sums = jnp.sum(probs, axis=-1, keepdims=True)
            probs = (probs * (1.0 / sums)).astype(BF16)
            attended[at, columns] = mm(probs, kv[:, HEAD:]).astype(BF16)
            logs = jnp.where(lane == h, top + jnp.log(sums), logs)
            tick(2 + heads * i + h)
        lse[at] = logs

    base = 2 + heads * (rows // block)

    @pl.loop(0, result.shape[1] // TILE)
    def _(n):
        tile_at(result, n)[...] = mm_t(attended[...], rows_at(w_out, n)[...]).astype(BF16)
        tick(base + n)

    for offset in range(1, count):
        passing(offset).wait_send()
    return base + result.shape[1] // TILE


def attention_forward_kernel(low, *refs):
    take = Taker(refs)
    gain, w_lin, w_out, bias = take(4)
    places_a, places_b = take(4), take(4)
    layer_a, layer_b = ab(take(1)[0])
    if not low:
        adds_a, adds_b, (last_b,) = (layer_a, *take(2)), (layer_b, *take(1)), take(1)
    outs_a, outs_b = zip(*[ab(ref) for ref in take(5)])
    if low:
        total_a, total_b = take(2)
    else:
        result_b, total_a, last_sum_b, layer = take(4)
        layer_a, layer_b = ab(layer)
    result_a, kv_sems_a, kv_sems_b = take(3)
    if low:
        (result_b,) = take(1)
    chain_a = Chain(result_a, total_a, *take(CHAIN_REFS))
    chain_b = Chain(result_b, total_b, *take(CHAIN_REFS)) if low else Chain(last_b, last_sum_b, *take(CHAIN_REFS))
    greet(kv_sems_a.shape[1])
    if not low:
        chain_b.start()

        def body(rows):
            layer_a[rows] = sum(ref[rows].astype(F32) for ref in adds_a).astype(BF16)

        by_rows(layer_a.shape[0], body)
    tick = ticker(None if low else chain_b, 0)
    done = attention_forward_stage(layer_a, gain, w_lin, w_out, bias, places_a, outs_a, result_a, kv_sems_a, tick)
    chain_a.start()
    if not low:
        chain_b.drain(done)
        chain_a.step(0)

        def body(rows):
            layer_b[rows] = sum(ref[rows].astype(F32) for ref in (*adds_b, last_sum_b)).astype(BF16)

        by_rows(layer_b.shape[0], body)
    taken = 0 if low else 1
    tick = ticker(chain_a, taken)
    done = attention_forward_stage(layer_b, gain, w_lin, w_out, bias, places_b, outs_b, result_b, kv_sems_b, tick)
    if low:
        chain_b.start()
    chain_a.drain(taken + done)
    if low:
        chain_b.drain(0)
    chain_a.settle()
    chain_b.settle()


def attention_forward(weights, places, inputs):
    w_lin, w_out, gains, bias = weights
    rows, width = inputs[0].shape[0] // 2, inputs[0].shape[1]
    q_cols = w_out.shape[1]
    keys = places[0][3].shape[1]
    count = keys // rows
    low = len(inputs) == 1
    narrow, both = jax.ShapeDtypeStruct((rows, width), BF16), jax.ShapeDtypeStruct((2 * rows, width), BF16)
    heads_out = jax.ShapeDtypeStruct((2 * rows, q_cols), BF16)
    kv_out = jax.ShapeDtypeStruct((2 * keys, 2 * HEAD), BF16)
    lse_out = jax.ShapeDtypeStruct((2 * rows, HEAD), F32)
    outs = [both, heads_out, kv_out, lse_out, heads_out] + ([narrow] * 2 if low else [narrow] * 3 + [both])
    args = (gains[:1], w_lin, w_out, bias, *places[0], *places[1], *inputs)
    return pl.pallas_call(
        functools.partial(attention_forward_kernel, low),
        out_shape=outs,
        in_specs=[VMEM] * len(args),
        out_specs=[VMEM] * len(outs),
        scratch_shapes=[pltpu.VMEM((rows, width), BF16)]
        + [pltpu.SemaphoreType.DMA((2, count))] * 2
        + [pltpu.VMEM((rows, width), BF16)] * low
        + chain_scratch((rows, width)) * 2,
        compiler_params=params(5 + low),
        cost_estimate=cost(),
    )(*args)


def attention_backward_stage(ins, sum_in, gain, w_lin, w_out, places, outs, gain_grad, result, scratch, tick):
    upstream, layer_in, attn_out, query, kv, lse, attended = ins
    cosine, sine, seg_rows, seg_keys = places
    attn_grad, lin = outs
    heads_grad, kv_grad, q_part, sent, got, kv_sems = scratch
    rows, q_cols = query.shape
    heads = q_cols // HEAD
    count = kv.shape[0] // rows
    me = lax.axis_index("ctx")
    block = min(256, rows)
    kv_grad[...] = jnp.zeros_like(kv_grad)
    norm_back_rows(
        upstream, sum_in, lambda r: layer_in[r].astype(F32) + attn_out[r].astype(F32), gain, gain_grad, attn_grad
    )
    tick(0)
    heads_grad[...] = mm(attn_grad[...], w_out[...]).astype(BF16)
    tick(1)

    @pl.loop(0, rows // block)
    def _(i):
        at = pl.ds(pl.multiple_of(i * block, block), block)
        allowed = allowed_keys(seg_rows, seg_keys, i, block)
        for h in range(heads):
            columns = slice(h * HEAD, (h + 1) * HEAD)
            scores = mm_t(query[at, columns], kv[:, :HEAD]) * SCALE - lse[at, h : h + 1]
            probs = jnp.exp(jnp.where(allowed, scores, NEG))
            grad = heads_grad[at, columns]
            row_sum = jnp.sum(attended[at, columns].astype(F32) * grad.astype(F32), axis=-1, keepdims=True)
            score_grad = (probs * (mm_t(grad, kv[:, HEAD:]) - row_sum)).astype(BF16)
            q_grad = mm(score_grad, kv[:, :HEAD]) * SCALE
            lin[at, columns] = unroped(q_grad, cosine[at], sine[at]).astype(BF16)
            kv_grad[:, :HEAD] += mm_0(score_grad, query[at, columns])
            kv_grad[:, HEAD:] += mm_0(probs.astype(BF16), grad)
            tick(2 + heads * i + h)

    def passing(offset):
        return pltpu.make_async_remote_copy(
            src_ref=sent.at[offset - 1],
            dst_ref=got.at[offset - 1],
            send_sem=kv_sems.at[0, offset],
            recv_sem=kv_sems.at[1, offset],
            device_id={"ctx": lax.rem(me + offset, count)},
            device_id_type=MESH,
        )

    for offset in range(1, count):
        peer = pl.ds(pl.multiple_of(lax.rem(me + offset, count) * rows, rows), rows)
        sent[offset - 1, :, :HEAD] = (kv_grad[peer, :HEAD] * SCALE).astype(BF16)
        sent[offset - 1, :, HEAD:] = kv_grad[peer, HEAD:].astype(BF16)
        passing(offset).start()
    base = 2 + heads * (rows // block)

    @pl.loop(0, result.shape[1] // TILE)
    def _(n):
        tile_at(q_part, n)[...] = mm_t(lin[:, :q_cols], rows_at(w_lin, n)[:, :q_cols])
        tick(base + n)

    mine = pl.ds(pl.multiple_of(me * rows, rows), rows)
    k_grad, v_grad = kv_grad[mine, :HEAD] * SCALE, kv_grad[mine, HEAD:]
    for offset in range(1, count):
        passing(offset).wait_recv()
        k_grad = k_grad + got[offset - 1, :, :HEAD].astype(F32)
        v_grad = v_grad + got[offset - 1, :, HEAD:].astype(F32)
    lin[:, q_cols : q_cols + HEAD] = unroped(k_grad, cosine[...], sine[...]).astype(BF16)
    lin[:, q_cols + HEAD :] = v_grad.astype(BF16)

    @pl.loop(0, result.shape[1] // TILE)
    def _(n):
        kv_part = mm_t(lin[:, q_cols:], rows_at(w_lin, n)[:, q_cols:])
        tile_at(result, n)[...] = (tile_at(q_part, n)[...] + kv_part).astype(BF16)


    for offset in range(1, count):
        passing(offset).wait_send()
    return base + result.shape[1] // TILE


def attention_backward_kernel(*refs):
    take = Taker(refs)
    gain, w_lin, w_out = take(3)
    places_a, places_b = take(4), take(4)
    ins_a, ins_b = zip(*[ab(ref) for ref in take(6)])
    attn_a, attn_b = take(2)
    ins_a, ins_b = (*ins_a[:2], attn_a, *ins_a[2:]), (*ins_b[:2], attn_b, *ins_b[2:])
    sum_a, last_b = take(2)
    outs_a, outs_b = zip(*[ab(ref) for ref in take(2)])
    gain_grad, result_b, total_a, total_b = take(4)
    heads_grad, kv_grad, q_part, result_a = take(4)
    exchange_a, exchange_b = take(3), take(3)
    chain_a = Chain(result_a, total_a, *take(CHAIN_REFS))
    chain_b = Chain(last_b, total_b, *take(CHAIN_REFS))
    greet(exchange_a[2].shape[1])
    chain_b.start()
    gain_grad[...] = jnp.zeros_like(gain_grad)
    scratch = (heads_grad, kv_grad, q_part, *exchange_a)
    done = attention_backward_stage(
        ins_a, sum_a, gain, w_lin, w_out, places_a, outs_a, gain_grad, result_a, scratch, ticker(chain_b, 0)
    )
    chain_a.start()
    chain_b.drain(done)
    chain_a.step(0)
    scratch = (heads_grad, kv_grad, q_part, *exchange_b)
    done = attention_backward_stage(
        ins_b, total_b, gain, w_lin, w_out, places_b, outs_b, gain_grad, result_b, scratch, ticker(chain_a, 1)
    )
    chain_a.drain(1 + done)
    chain_a.settle()
    chain_b.settle()


def attention_backward(upstream, sum_a, last_b, kept, weights, places):
    w_lin, w_out, gains, bias = weights
    rows, width = sum_a.shape
    q_cols = w_out.shape[1]
    keys = places[0][3].shape[1]
    count = keys // rows
    narrow = jax.ShapeDtypeStruct((rows, width), BF16)
    both = jax.ShapeDtypeStruct((2 * rows, width), BF16)
    lin_out = jax.ShapeDtypeStruct((2 * rows, q_cols + 2 * HEAD), BF16)
    outs = [both, lin_out] + [jax.ShapeDtypeStruct((8, width), F32)] + [narrow] * 3
    names = ("layer_in", "query", "kv", "lse", "attended", "attn_a", "attn_b")
    args = (gains[1:], w_lin, w_out, *places[0], *places[1], upstream)
    args += (*[kept[name] for name in names], sum_a, last_b)
    exchange = [pltpu.VMEM((max(count - 1, 1), rows, 2 * HEAD), BF16)] * 2 + [pltpu.SemaphoreType.DMA((2, count))]
    return pl.pallas_call(
        attention_backward_kernel,
        out_shape=outs,
        in_specs=[VMEM] * len(args),
        out_specs=[VMEM] * len(outs),
        scratch_shapes=[
            pltpu.VMEM((rows, q_cols), BF16),
            pltpu.VMEM((keys, 2 * HEAD), F32),
            pltpu.VMEM((rows, width), F32),
            pltpu.VMEM((rows, width), BF16),
        ]
        + exchange * 2
        + chain_scratch((rows, width)) * 2,
        compiler_params=params(7),
        cost_estimate=cost(),
    )(*args)


def rope_tables(places):
    steps = jnp.arange(HEAD // 2, dtype=F32) * (2.0 / HEAD)
    inverse = ROPE_BASE ** (-steps)
    angles = places.astype(F32)[..., None] * inverse
    angles = jnp.concatenate([angles, angles], axis=-1)
    return (jnp.cos(angles), jnp.sin(angles))


def over_ctx(value):
    if lax.axis_size("ctx") == 2:
        other = lax.ppermute(value, "ctx", [(0, 1), (1, 0)])
        low = lax.axis_index("ctx") == 0
        return jnp.concatenate([jnp.where(low, value, other), jnp.where(low, other, value)], axis=-1)
    return lax.all_gather(value, "ctx", axis=value.ndim - 1, tiled=True)


def local(
    section_in,
    segments,
    positions,
    query_weight,
    kv_weight,
    output_weight,
    gate_up,
    down_weight,
    norm_gains,
    query_bias,
    kv_bias,
    out_grad,
):
    sec = lax.axis_index("section")
    first = sec == 0
    group = HEADS // KV_HEADS
    heads_here = HEADS // lax.axis_size("tp")
    head_pick = lax.axis_index("tp") * heads_here // group
    shards = lax.axis_size("dp") * lax.axis_size("ctx")
    ranks = ("dp", "ctx")
    seqs, span, width = section_in.shape[1:]
    shard = query_weight.shape[1]
    q_cols = query_weight.shape[2]
    ff = gate_up.shape[3]

    def per_layer(mine, theirs):
        return jnp.where(first, mine, theirs), jnp.where(first, theirs, mine)

    half = shard // 2
    kv_width = KV_HEADS * HEAD

    def halves(rows):
        mine = lax.dynamic_slice_in_dim(rows, sec * half, half, 0)
        return per_layer(mine, swap(lax.dynamic_slice_in_dim(rows, (1 - sec) * half, half, 0)))

    def joined(own):
        return jnp.stack(per_layer(own, swap(own)), axis=1).reshape(width, own.shape[-1])

    def after(value, event):
        return lax.optimization_barrier((value, event))[0]

    piece = HEAD // shards
    biases = jnp.concatenate([query_bias[0].reshape(-1), kv_bias[0].reshape(-1)])
    n_biases = biases.shape[0]
    biases = jnp.pad(biases, (0, -n_biases % shard)).reshape(-1, shard).T
    extra = jnp.concatenate([norm_gains[0].T, biases], axis=1)
    n_extra = extra.shape[1]
    extra = jnp.pad(extra, ((0, 0), (0, HEAD - n_extra)))
    packed = jnp.concatenate([query_weight[0], kv_weight[0, 0], kv_weight[0, 1], output_weight[0].T, extra], axis=1)
    packed_shards = halves(packed)
    first_shard, gate_up, down_weight, positions, segments, section_in = lax.optimization_barrier(
        (packed_shards[0], gate_up, down_weight, positions, segments, section_in)
    )
    packed_low = lax.all_gather(first_shard, ranks, axis=0)
    spare = -ff % TILE
    wide = jnp.pad(gate_up[0], ((0, 0), (0, 0), (0, spare)))
    mine = lax.dynamic_index_in_dim(wide, sec, 0, keepdims=False)
    theirs = swap(lax.dynamic_index_in_dim(wide, 1 - sec, 0, keepdims=False))
    gate_up_shards = per_layer(mine, theirs)
    down_shards = halves(jnp.pad(down_weight[0].T, ((0, 0), (0, spare))))

    micro = sec
    seg = lax.dynamic_index_in_dim(segments, micro, 0, keepdims=False)
    pos = lax.dynamic_index_in_dim(positions, micro, 0, keepdims=False)
    hidden = lax.dynamic_index_in_dim(section_in, micro, 0, keepdims=False)
    seg_keys = over_ctx(seg)
    segs, tables = [], []
    for q in range(seqs):
        segs.append((seg[q][:, None], seg_keys[q][None]))
        cosine, sine = rope_tables(pos[q])
        tables.append((cosine, jnp.where(jnp.arange(HEAD) < HEAD // 2, -sine, sine)))
    hidden = hidden.reshape(seqs * span, width)

    packed_low, gate_up_shards, down_shards, packed_shards, segs, tables, hidden = lax.optimization_barrier(
        (packed_low, gate_up_shards, down_shards, packed_shards, segs, tables, hidden)
    )
    own_low = lax.all_gather(gate_up_shards[0], ranks, axis=0, tiled=True)
    down_low = lax.all_gather(down_shards[0], ranks, axis=0)

    def attention_weights(own):
        p = joined(own)
        wq = p[:, :q_cols]
        wk = lax.dynamic_slice_in_dim(p[:, q_cols : q_cols + kv_width], head_pick * HEAD, HEAD, 1)
        wv = lax.dynamic_slice_in_dim(p[:, q_cols + kv_width : q_cols + 2 * kv_width], head_pick * HEAD, HEAD, 1)
        wo = p[:, q_cols + 2 * kv_width : 2 * q_cols + 2 * kv_width]
        s = p[:, 2 * q_cols + 2 * kv_width :]
        gains = s[:, :2].T
        s = s[:, 2:n_extra].T.reshape(-1, shards, shard).transpose(1, 0, 2).reshape(shards, -1)[:, :n_biases]
        q_b = s[:, : heads_here * piece].reshape(shards, heads_here, piece).transpose(1, 0, 2).reshape(heads_here, HEAD)
        kv_b = s[:, heads_here * piece :].reshape(shards, 2, KV_HEADS, piece)
        kv_b = kv_b.transpose(1, 2, 0, 3).reshape(2, KV_HEADS, HEAD)
        kv_b = lax.dynamic_slice_in_dim(kv_b, head_pick, 1, 1)
        bias = jnp.concatenate([q_b.reshape(1, -1), kv_b.reshape(1, -1)], axis=1).astype(F32)
        return jnp.concatenate([wq, wk, wv], axis=1), wo, gains.astype(F32), bias

    names = ("layer_in", "query", "kv", "lse", "attended", "attn_a", "attn_b")
    args = (gains[1:], w_lin, w_out, *places[0], *places[1], upstream)
    args += (*[kept[name] for name in names], sum_a, last_b)
    exchange = [pltpu.VMEM((max(count - 1, 1), rows, 2 * HEAD), BF16)] * 2 + [pltpu.SemaphoreType.DMA((2, count))]
    return pl.pallas_call(
        attention_backward_kernel,
        out_shape=outs,
        in_specs=[VMEM] * len(args),
        out_specs=[VMEM] * len(outs),
        scratch_shapes=[
            pltpu.VMEM((rows, q_cols), BF16),
            pltpu.VMEM((keys, 2 * HEAD), F32),
            pltpu.VMEM((rows, width), F32),
            pltpu.VMEM((rows, width), BF16),
        ]
        + exchange * 2
        + chain_scratch((rows, width)) * 2,
        compiler_params=params(7),
        cost_estimate=cost(),
    )(*args)


def rope_tables(places):
    steps = jnp.arange(HEAD // 2, dtype=F32) * (2.0 / HEAD)
    inverse = ROPE_BASE ** (-steps)
    angles = places.astype(F32)[..., None] * inverse
    angles = jnp.concatenate([angles, angles], axis=-1)
    return (jnp.cos(angles), jnp.sin(angles))


def norm_back(grad_out, rows_in, factor, gain):
    unit = rows_in * factor
    gain_grad = jnp.sum(grad_out * unit, axis=0)
    weighted = grad_out * gain
    return (
        factor * (weighted - unit * jnp.mean(weighted * unit, axis=-1, keepdims=True)),
        gain_grad,
    )


def over_ctx(value):
    if lax.axis_size("ctx") == 2:
        other = lax.ppermute(value, "ctx", [(0, 1), (1, 0)])
        low = lax.axis_index("ctx") == 0
        return jnp.concatenate([jnp.where(low, value, other), jnp.where(low, other, value)], axis=-1)
    return lax.all_gather(value, "ctx", axis=value.ndim - 1, tiled=True)


def input_backward(normed_one_grad, middle_grad, kept, gains):
    layer_in = kept["layer_in"].astype(F32)
    factor = lax.rsqrt(jnp.mean(layer_in * layer_in, axis=-1, keepdims=True) + EPS)
    norm_grad, gain_one = norm_back(normed_one_grad.astype(F32), layer_in, factor, gains[0])
    return (middle_grad.astype(F32) + norm_grad).astype(BF16), gain_one


def local(
    section_in,
    segments,
    positions,
    query_weight,
    kv_weight,
    output_weight,
    gate_up,
    down_weight,
    norm_gains,
    query_bias,
    kv_bias,
    out_grad,
):
    sec = lax.axis_index("section")
    first = sec == 0
    group = HEADS // KV_HEADS
    heads_here = HEADS // lax.axis_size("tp")
    head_pick = lax.axis_index("tp") * heads_here // group
    shards = lax.axis_size("dp") * lax.axis_size("ctx")
    ranks = ("dp", "ctx")
    seqs, span, width = section_in.shape[1:]
    shard = query_weight.shape[1]
    q_cols = query_weight.shape[2]
    ff = gate_up.shape[3]

    def per_layer(mine, theirs):
        return jnp.where(first, mine, theirs), jnp.where(first, theirs, mine)

    half = shard // 2
    kv_width = KV_HEADS * HEAD

    def halves(rows):
        mine = lax.dynamic_slice_in_dim(rows, sec * half, half, 0)
        return per_layer(mine, swap(lax.dynamic_slice_in_dim(rows, (1 - sec) * half, half, 0)))

    def joined(own):
        return jnp.stack(per_layer(own, swap(own)), axis=1).reshape(width, own.shape[-1])

    def after(value, event):
        return lax.optimization_barrier((value, event))[0]

    piece = HEAD // shards
    biases = jnp.concatenate([query_bias[0].reshape(-1), kv_bias[0].reshape(-1)])
    n_biases = biases.shape[0]
    biases = jnp.pad(biases, (0, -n_biases % shard)).reshape(-1, shard).T
    extra = jnp.concatenate([norm_gains[0].T, biases], axis=1)
    n_extra = extra.shape[1]
    extra = jnp.pad(extra, ((0, 0), (0, HEAD - n_extra)))
    packed = jnp.concatenate([query_weight[0], kv_weight[0, 0], kv_weight[0, 1], output_weight[0].T, extra], axis=1)
    packed_shards = halves(packed)
    first_shard, gate_up, down_weight, positions, segments, section_in = lax.optimization_barrier(
        (packed_shards[0], gate_up, down_weight, positions, segments, section_in)
    )
    packed_low = lax.all_gather(first_shard, ranks, axis=0)
    spare = -ff % TILE
    wide = jnp.pad(gate_up[0], ((0, 0), (0, 0), (0, spare)))
    mine = lax.dynamic_index_in_dim(wide, sec, 0, keepdims=False)
    theirs = swap(lax.dynamic_index_in_dim(wide, 1 - sec, 0, keepdims=False))
    gate_up_shards = per_layer(mine, theirs)
    down_shards = halves(jnp.pad(down_weight[0].T, ((0, 0), (0, spare))))

    micro = sec
    seg = lax.dynamic_index_in_dim(segments, micro, 0, keepdims=False)
    pos = lax.dynamic_index_in_dim(positions, micro, 0, keepdims=False)
    hidden = lax.dynamic_index_in_dim(section_in, micro, 0, keepdims=False)
    seg_keys = over_ctx(seg)
    segs, tables = [], []
    for q in range(seqs):
        segs.append((seg[q][:, None], seg_keys[q][None]))
        cosine, sine = rope_tables(pos[q])
        tables.append((cosine, jnp.where(jnp.arange(HEAD) < HEAD // 2, -sine, sine)))
    hidden = hidden.reshape(seqs * span, width)

    packed_low, gate_up_shards, down_shards, packed_shards, segs, tables, hidden = lax.optimization_barrier(
        (packed_low, gate_up_shards, down_shards, packed_shards, segs, tables, hidden)
    )
    own_low = lax.all_gather(gate_up_shards[0], ranks, axis=0, tiled=True)
    down_low = lax.all_gather(down_shards[0], ranks, axis=0)

    def attention_weights(own):
        p = joined(own)
        wq = p[:, :q_cols]
        wk = lax.dynamic_slice_in_dim(p[:, q_cols : q_cols + kv_width], head_pick * HEAD, HEAD, 1)
        wv = lax.dynamic_slice_in_dim(p[:, q_cols + kv_width : q_cols + 2 * kv_width], head_pick * HEAD, HEAD, 1)
        wo = p[:, q_cols + 2 * kv_width : 2 * q_cols + 2 * kv_width]
        s = p[:, 2 * q_cols + 2 * kv_width :]
        gains = s[:, :2].T
        s = s[:, 2:n_extra].T.reshape(-1, shards, shard).transpose(1, 0, 2).reshape(shards, -1)[:, :n_biases]
        q_b = s[:, : heads_here * piece].reshape(shards, heads_here, piece).transpose(1, 0, 2).reshape(heads_here, HEAD)
        kv_b = s[:, heads_here * piece :].reshape(shards, 2, KV_HEADS, piece)
        kv_b = kv_b.transpose(1, 2, 0, 3).reshape(2, KV_HEADS, HEAD)
        kv_b = lax.dynamic_slice_in_dim(kv_b, head_pick, 1, 1)
        bias = jnp.concatenate([q_b.reshape(1, -1), kv_b.reshape(1, -1)], axis=1).astype(F32)
        return jnp.concatenate([wq, wk, wv], axis=1), wo, gains.astype(F32), bias

    kept = [[dict(), dict()] for _ in range(2)]
    names = ("normed", "query", "kv", "lse", "attended")
    more_names = ("normed_two", "gate", "up", "inner")
    attn_weights, ffn_weights = [attention_weights(packed_low), None], [None, None]
    places = [(*tables[q], *segs[q]) for q in range(seqs)]

    def keep(layer, names, values):
        kept[layer].update(zip(names, values))
        return values[len(names) :]

    kept = [dict(), dict()]
    attn_a, attn_b = keep(0, names, attention_forward(attn_weights[0], places, (hidden,)))
    kept[0].update(layer_in=hidden, attn_a=attn_a, attn_b=attn_b)
    attn_b, own_low, down_low = lax.optimization_barrier((attn_b, own_low, down_low))
    ffn_weights[0] = own_low, down_low
    packed_high = lax.all_gather(after(packed_shards[1], attn_b), ranks, axis=0)
    own_high = lax.all_gather(after(gate_up_shards[1], attn_b), ranks, axis=0, tiled=True)
    down_high = lax.all_gather(after(down_shards[1], attn_b), ranks, axis=0)
    gain = attn_weights[0][2][1:]
    part_b, ffn_a = keep(
        0, more_names, ffn_forward(False, hidden, attn_a, attn_b, gain, ffn_weights[0])
    )

    packed_high, part_b = lax.optimization_barrier((packed_high, part_b))
    attn_weights[1] = attention_weights(packed_high)
    inputs = (hidden, attn_a, ffn_a, attn_b, part_b)
    part_b, attn_a, _, layer_in = keep(1, names, attention_forward(attn_weights[1], places, inputs))
    part_b, own_high, down_high = lax.optimization_barrier((part_b, own_high, down_high))
    ffn_weights[1] = own_high, down_high
    gain = attn_weights[1][2][1:]
    part_b, ffn_a, attn_b = keep(
        1, more_names, ffn_forward(True, layer_in, attn_a, part_b, gain, ffn_weights[1])
    )
    kept[1].update(layer_in=layer_in, attn_a=attn_a, attn_b=attn_b)
    upstream = lax.dynamic_index_in_dim(out_grad, micro, 0, keepdims=False).reshape(seqs * span, width)
    k = kept[1]
    *wide_grads, grad_b, sum_a, ffn_b = ffn_backward(upstream, k["gate"], k["up"], ffn_weights[1], part_b)
    attn_sum, ffn_sum = jnp.concatenate([attn_a, attn_b]), jnp.concatenate([ffn_a, ffn_b])
    outs = [layer_in, (layer_in.astype(F32) + attn_sum.astype(F32) + ffn_sum.astype(F32)).astype(BF16)]

    def to_section(values):
        low = lax.ppermute(values[0], "section", [(1, 0)])
        high = lax.ppermute(values[1], "section", [(0, 1)])
        both = jnp.stack([jnp.where(first, values[0], high), jnp.where(first, low, values[1])])
        return both.reshape(2, seqs, span, width)

    section_out = to_section(outs)

    in_grads = [None, None]
    gate_up_grads, down_grads, packed_grads, gains_grads = [[None, None] for _ in range(4)]
    for layer in (1, 0):
        weights, k = attn_weights[layer], kept[layer]
        if layer == 0:
            below = (sum_a, kept[1]["layer_in"], attn_weights[1][2][:1])
            *wide_grads, grad_b, sum_a, _, upstream, gain_one = ffn_backward(
                attn_grad, k["gate"], k["up"], ffn_weights[0], part_b, below
            )
            in_grads[1] = upstream
            gains_grads[1] = jnp.stack([jnp.sum(gain_one, axis=0), gain_two])
            sum_a, gate_up_grads[1] = lax.optimization_barrier((sum_a, gate_up_grads[1]))
        own_w, other_w = [dot("rd,rf->df", k["normed_two"], g).astype(BF16) for g in wide_grads]
        own_w = (own_w.astype(F32) + swap(other_w).astype(F32)).astype(BF16)
        down_w = dot("rd,rf->df", upstream, k["inner"]).astype(BF16)
        down_w = down_w.reshape(shards, 2, half, ff + spare)
        down_own = lax.dynamic_index_in_dim(down_w, sec, 1, keepdims=False)
        down_other = lax.dynamic_index_in_dim(down_w, 1 - sec, 1, keepdims=False)
        down_own = (down_own.astype(F32) + swap(down_other).astype(F32)).astype(BF16)
        own_w, down_own, sum_a = lax.optimization_barrier((own_w, down_own, sum_a))
        gate_up_grads[layer] = lax.psum_scatter(own_w, ranks, scatter_dimension=0, tiled=True)
        down_grads[layer] = lax.psum_scatter(
            down_own.reshape(shards * half, ff + spare), ranks, scatter_dimension=0, tiled=True
        )

        attn_grad, lin_grad, gain_two, part_b, sum_a, _ = attention_backward(upstream, sum_a, grad_b, k, weights, places)
        gain_two = jnp.sum(gain_two, axis=0)
        if layer == 0:
            part_b, down_grads[1] = lax.optimization_barrier((part_b, down_grads[1]))
        lin_w = dot("rd,re->de", k["normed"], lin_grad)
        out_w = dot("rd,re->de", attn_grad, k["attended"])
        bias = jnp.sum(lin_grad.astype(F32), axis=0)
        bias = bias.reshape(heads_here + 2, shards, piece).transpose(1, 0, 2).reshape(shards, (heads_here + 2) * piece)
        bias = jnp.pad(bias, ((0, 0), (0, -bias.shape[1] % shard)))
        bias = bias.reshape(shards, -1, shard).transpose(0, 2, 1).reshape(width, -1)
        bias = jnp.pad(bias, ((0, 0), (0, HEAD - bias.shape[1])))
        packed_grads[layer] = jnp.concatenate([lin_w, out_w, bias], axis=1).astype(BF16)

    low = lax.ppermute(packed_grads[0], "section", [(1, 0)])
    high = lax.ppermute(packed_grads[1], "section", [(0, 1)])
    packed_total = jnp.where(
        first, packed_grads[0].astype(F32) + low.astype(F32), packed_grads[1].astype(F32) + high.astype(F32)
    ).astype(BF16)
    last_part, gate_up_grads[0], down_grads[0], packed_total = lax.optimization_barrier(
        (part_b, gate_up_grads[0], down_grads[0], packed_total)
    )
    packed_total = lax.psum_scatter(packed_total, ranks, scatter_dimension=0, tiled=True).astype(F32)
    in_grads[0], gain_one = last_grads(last_part, sum_a, attn_grad, kept[0]["layer_in"], attn_weights[0][2][:1])
    gains_grads[0] = jnp.stack([jnp.sum(gain_one, axis=0), gain_two])
    input_grad = to_section(in_grads)
    low = lax.ppermute(gains_grads[0], "section", [(1, 0)])
    high = lax.ppermute(gains_grads[1], "section", [(0, 1)])
    gains_grad = jnp.where(first, gains_grads[0] + low, gains_grads[1] + high)
    for axis in ranks:
        if lax.axis_size(axis) == 2:
            gains_grad = gains_grad + lax.ppermute(gains_grad, axis, [(0, 1), (1, 0)])
        else:
            gains_grad = lax.psum(gains_grad, axis)
    at = (lax.axis_index("dp") * lax.axis_size("ctx") + lax.axis_index("ctx")) * shard
    gains_grad = lax.dynamic_slice_in_dim(gains_grad, at, shard, 1)
    q_grad = packed_total[:, :q_cols]
    kv_narrow = packed_total[:, q_cols : q_cols + 2 * HEAD].reshape(shard, 2, HEAD)
    o_grad = packed_total[:, q_cols + 2 * HEAD : 2 * q_cols + 2 * HEAD].T
    extra = packed_total[:, 2 * q_cols + 2 * HEAD :]
    bias_cols = -(-(heads_here + 2) * piece // shard)
    bias = extra[:, :bias_cols].T.reshape(-1)[: (heads_here + 2) * piece].reshape(heads_here + 2, piece)
    q_bias_grad = bias[:heads_here]
    kv_bias = bias[heads_here:].reshape(1, -1)
    kv_bias = jnp.pad(kv_bias, ((0, 15), (0, -kv_bias.shape[1] % (2 * HEAD))))
    mine = jnp.concatenate([kv_narrow.reshape(shard, 2 * HEAD), kv_bias[:, : 2 * HEAD]]).astype(BF16)
    mine = (mine.astype(F32) + lax.ppermute(mine, "tp", [(0, 1), (1, 0), (2, 3), (3, 2)]).astype(F32)).astype(BF16)
    theirs = lax.ppermute(mine, "tp", [(0, 2), (2, 0), (1, 3), (3, 1)])
    mine, theirs = mine.astype(F32), theirs.astype(F32)
    low = head_pick == 0
    heads = jnp.stack([jnp.where(low, mine, theirs), jnp.where(low, theirs, mine)])
    kv_grad = heads[:, :shard].reshape(KV_HEADS, shard, 2, HEAD).transpose(2, 1, 0, 3).reshape(2, shard, KV_HEADS * HEAD)
    kv_bias_grad = heads[:, shard, : 2 * piece].reshape(KV_HEADS, 2, piece).transpose(1, 0, 2)

    def collect(values):
        kept_half = jnp.where(first, values[0], values[1])
        other = swap(jnp.where(first, values[1], values[0]))
        return jnp.where(first, kept_half, other), jnp.where(first, other, kept_half)

    gate_up_grad = jnp.stack(collect(gate_up_grads))[..., :ff].astype(F32)
    down_grad = jnp.concatenate(collect(down_grads), axis=0)[:, :ff].T.astype(F32)
    return (
        section_out[None],
        input_grad[None],
        q_grad[None],
        kv_grad[None],
        o_grad[None],
        gate_up_grad[None],
        down_grad[None],
        gains_grad[None],
        q_bias_grad[None],
        kv_bias_grad[None],
    )


def solution(mesh):
    in_specs = (
        P(None, "dp", "ctx", None),
        P(None, "dp", "ctx"),
        P(None, "dp", "ctx"),
        P("section", ("dp", "ctx"), "tp"),
        P("section", None, ("dp", "ctx"), None),
        P("section", "tp", ("dp", "ctx")),
        P("section", None, ("dp", "ctx"), "tp"),
        P("section", "tp", ("dp", "ctx")),
        P("section", None, ("dp", "ctx")),
        P("section", "tp", ("dp", "ctx")),
        P("section", None, None, ("dp", "ctx")),
        P(None, "dp", "ctx", None),
    )
    out_specs = (
        P("section", None, "dp", "ctx", None),
        P("section", None, "dp", "ctx", None),
        P("section", ("dp", "ctx"), "tp"),
        P("section", None, ("dp", "ctx"), None),
        P("section", "tp", ("dp", "ctx")),
        P("section", None, ("dp", "ctx"), "tp"),
        P("section", "tp", ("dp", "ctx")),
        P("section", None, ("dp", "ctx")),
        P("section", "tp", ("dp", "ctx")),
        P("section", None, None, ("dp", "ctx")),
    )
    return jax.shard_map(local, mesh=mesh, in_specs=in_specs, out_specs=out_specs, check_vma=False)
```

profile of v0, /device:TPU:0, one launch (start us, length us, event | category | flops | bytes accessed | tf_op | source)
XLA Modules:
  0.0 1163.4 jit_solution(9017443541117332459)
XLA Ops:
  17.8 2.9 collective-permute-start.3
  20.7 3.5 pad_dynamic-slice_fusion.1
  24.2 2.3 copy.119
  29.4 2.8 negate_select_fusion
  32.3 3.8 constant_dynamic-slice_fusion.12
  36.0 2.7 copy.118
  40.0 2.7 broadcast_select_fusion.10
  42.7 3.5 bitcast_select_fusion
  46.2 17.9 %all-gather.15.cloned.1.call-done = bf16[768,1408]{1,0:T(8,128)(2,1)} async-done(((bf16[192,1408]{1,0:T(8,128)(2,1)}), bf16[768,1408]{1,0:T(8,128)(2,1)}) %all-gather.15.cloned.1.call-update) | async-done | bytes 2162704 | tf_op jit(solution)/shard_map/all_gather | solution.py:1150
  66.8 2.8 collective-permute-done.4
  82.7 110.9 %shard_map.195 = (bf16[1024,1536]{1,0:T(8,128)(2,1)}, bf16[1024,384]{1,0:T(8,128)(2,1)}, bf16[2048,256]{1,0:T(8,128)(2,1)}, f32[1024,128]{1,0:T(8,128)}, bf16[10...) custom-call(f32[1,1536]{1,0:T(1,128)} %get-tuple-element.281.refs_0_.gain, ...), custom_call_target="tpu_custom_call" | custom-call | flops 1048576 | bytes 1048576 | tf_op jit(solution)/shard_map/pallas_call | solution.py:773
  193.7 6.6 all-gather.11.cloned.1.call-done.refs_4_
  201.5 75.2 %shard_map.196 = (bf16[1024,1536]{1,0:T(8,128)(2,1)}, bf16[1024,2304]{1,0:T(8,128)(2,1)}, bf16[1024,2304]{1,0:T(8,128)(2,1)}, bf16[1024,2304]{1,0:T(8,128)(2,1)}...) custom-call(bf16[1024,1536]{1,0:T(8,128)(2,1)} %bitcast.159, ...), custom_call_target="tpu_custom_call" | custom-call | flops 1048576 | bytes 1048576 | tf_op jit(solution)/shard_map/pallas_call | solution.py:458
  276.9 3.9 constant_dynamic-slice_fusion.5
  292.7 105.2 %shard_map.197 = (bf16[1024,1536]{1,0:T(8,128)(2,1)}, bf16[1024,384]{1,0:T(8,128)(2,1)}, bf16[2048,256]{1,0:T(8,128)(2,1)}, f32[1024,128]{1,0:T(8,128)}, bf16[10...) custom-call(f32[1,1536]{1,0:T(1,128)} %get-tuple-element.279.refs_0_, ...), custom_call_target="tpu_custom_call" | custom-call | flops 1048576 | bytes 1048576 | tf_op jit(solution)/shard_map/pallas_call | solution.py:773
  397.9 90.1 %shard_map.198 = (bf16[1024,1536]{1,0:T(8,128)(2,1)}, bf16[1024,2304]{1,0:T(8,128)(2,1)}, bf16[1024,2304]{1,0:T(8,128)(2,1)}, bf16[1024,2304]{1,0:T(8,128)(2,1)}...) custom-call(bf16[1024,1536]{1,0:T(8,128)(2,1)} %get-tuple-element.136.refs_0_.refs_12_.refs_7_, ...), custom_call_target="tpu_custom_call" | custom-call | flops 1048576 | bytes 1048576 | tf_op jit(solution)/shard_map/pallas_call | solution.py:458
  488.1 90.2 %shard_map.199 = (bf16[1024,2304]{1,0:T(8,128)(2,1)}, bf16[1024,2304]{1,0:T(8,128)(2,1)}, bf16[512,1536]{1,0:T(8,128)(2,1)}, bf16[512,1536]{1,0:T(8,128)(2,1)}, bf16[512,1536]{1,0:T(8,128)(2,1)}) custom-call(bf16[1024,1536]{1,0:T(8,128)(2,1)} %bitcast.163, bf16[512,1536]{1,0:T(8,128)(2,1)} %get-tuple-element.148.refs_1_, ...), custom_call_target="tpu_custom_call" | custom-call | flops 1048576 | bytes 1048576 | tf_op jit(solution)/shard_map/pallas_call | solution.py:586
  578.3 10.5 convolution_convert_fusion.4
  588.8 10.3 convolution_convert_fusion.3
  600.0 5.8 collective-permute-done.9
  605.8 2.7 fusion.3
  608.5 11.9 %add_convert_fusion.1 = bf16[1536,2304]{1,0:T(8,128)(2,1)} fusion(bf16[1536,2304]{1,0:T(8,128)(2,1)S(1)} %collective-permute-done.8, bf16[1024,1536]{1,0:T(8,128)(2,1)S(1)} %copy-done.30, bf16[1024,2304]{1,0:T(8,128)(2,1)} %get-tuple-element.157), kind=kOutput, calls=%fused_computation.1 | convolution fusion | flops 7265452032 | bytes 22020096 | tf_op jit(solution)/shard_map/rd,rf->df/dot_general | solution.py:27
  620.4 102.0 %shard_map.200 = (bf16[1024,1536]{1,0:T(8,128)(2,1)}, bf16[1024,640]{1,0:T(8,128)(2,1)}, f32[8,1536]{1,0:T(8,128)}, bf16[512,1536]{1,0:T(8,128)(2,1)}, bf16[512,...) custom-call(f32[1,1536]{1,0:T(1,128)} %get-tuple-element.278.refs_3_.refs_0_, bf16[1536,640]{1,0:T(8,128)(2,1)} %pad_maximum_fusion.6.refs_1_, ...), custom_call_target="tpu_custom_call" | custom-call | flops 1048576 | bytes 1048576 | tf_op jit(solution)/shard_map/pallas_call | solution.py:911
  722.5 92.4 %shard_map.201 = (bf16[1024,2304]{1,0:T(8,128)(2,1)}, bf16[1024,2304]{1,0:T(8,128)(2,1)}, bf16[512,1536]{1,0:T(8,128)(2,1)}, bf16[512,1536]{1,0:T(8,128)(2,1)}, ...) custom-call(bf16[1024,1536]{1,0:T(8,128)(2,1)} %get-tuple-element.163.refs_0_, ...), custom_call_target="tpu_custom_call" | custom-call | flops 1048576 | bytes 1048576 | tf_op jit(solution)/shard_map/pallas_call | solution.py:586
  814.9 11.7 %convolution_convert_fusion.1 = bf16[1536,2304]{1,0:T(8,128)(2,1)} fusion(bf16[1024,1536]{1,0:T(8,128)(2,1)S(1)} %copy-done.28, bf16[1024,2304]{1,0:T(8,128)(2,1)} %get-tuple-element.175), kind=kOutput, calls=%fused_computation.3 | convolution fusion | flops 7251296256 | bytes 14942208 | tf_op jit(solution)/shard_map/rd,rf->df/dot_general | solution.py:27
  827.1 10.6 convolution_convert_fusion
  838.6 5.8 collective-permute-done.11
  844.4 2.7 fusion.2
  847.1 11.3 add_convert_fusion
  861.6 6.3 collective-permute-done.7
  867.9 5.6 broadcast_select_fusion.2
  873.5 3.8 collective-permute-start.6
  879.0 3.7 convolution_convert_fusion.8
  887.5 3.1 collective-permute-start.13
  890.6 102.5 %shard_map.202 = (bf16[1024,1536]{1,0:T(8,128)(2,1)}, bf16[1024,640]{1,0:T(8,128)(2,1)}, f32[8,1536]{1,0:T(8,128)}, bf16[512,1536]{1,0:T(8,128)(2,1)}, bf16[512,...) custom-call(f32[1,1536]{1,0:T(1,128)} %get-tuple-element.280.refs_3_.refs_0_, bf16[1536,640]{1,0:T(8,128)(2,1)} %pad_maximum_fusion.5.refs_1_, ...), custom_call_target="tpu_custom_call" | custom-call | flops 1048576 | bytes 1048576 | tf_op jit(solution)/shard_map/pallas_call | solution.py:911
  995.0 3.7 convolution_convert_fusion.9
  1006.8 8.4 collective-permute-start.14
  1015.2 5.6 select_convert_fusion
  1020.9 3.7 copy.148
  1026.5 5.2 pad_maximum_fusion
  1034.8 54.1 %shard_map.203 = (bf16[1024,1536]{1,0:T(8,128)(2,1)}, f32[8,1536]{1,0:T(8,128)}) custom-call(bf16[512,1536]{1,0:T(8,128)(2,1)} %get-tuple-element.192.part, bf16[512,1536]{1,0:T(8,128)(2,1)} %get-tuple-element.193.sum_a, bf16[1024,1536]{1,0:T(8,128)(2,1)} %get-tuple-element.189.grad, bf16[1024,1536]{1,0:T(8,128)(2,1)} %bitcast.162, ...), custom_call_target="tpu_custom_call" | custom-call | flops 1048576 | bytes 1048576 | tf_op jit(solution)/shard_map/pallas_call | solution.py:618
  1101.0 4.1 broadcast_select_fusion.1
  1106.1 2.9 copy.146
  1111.4 3.4 fusion.7
  1114.7 7.9 copy.145
  1122.7 4.0 broadcast_select_fusion
  1130.9 5.2 pad_maximum_fusion.1
  1140.9 12.5 %collective-permute-done.17 = bf16[400,256]{0,1:T(8,128)(2,1)S(1)} collective-permute-done((bf16[400,256]{0,1:T(8,128)(2,1)S(1)}, bf16[400,256]{0,1:T(8,128)(2,1)S(1)}, u32[]{:S(2)}, u32[]{:S(2)}) %collective-permute-start.17) | collective-permute-done | bytes 204832 | tf_op jit(solution)/shard_map/ppermute | solution.py:1311
  (265 shorter events, 97.6 us)
Async XLA Ops:
  7.2 10.0 copy-start.25
  7.2 56.9 %all-gather.15.cloned.1.call-start = ((), (), s32[]{:S(2)}) async-start(), calls=%async_computation.11 | async-start | bytes 2703360 | tf_op jit(solution)/shard_map/all_gather | solution.py:1150
  14.0 2.1 collective-permute-start
  17.8 20.9 %collective-permute-start.3 = (s32[2,512]{1,0:T(2,128)}, s32[2,512]{1,0:T(2,128)}, u32[]{:S(2)}, u32[]{:S(2)}) collective-permute-start(s32[2,512]{1,0:T(2,128)} %fusion.16), channel_id=1, source_target_pairs={{0,4},{4,0},{1,5},{5,1},{2,6},{6,2},{3,7},{7,3},{8,12},{12,8},{9,1... | collective-permute-start | bytes 12296 | tf_op jit(solution)/shard_map/ppermute | solution.py:1083
  26.5 16.2 %collective-permute-start.1 = (bf16[384,2304]{1,0:T(8,128)(2,1)}, bf16[384,2304]{1,0:T(8,128)(2,1)}, u32[]{:S(2)}, u32[]{:S(2)}) collective-permute-start(bf16[384,2304]{1,0:T(8,128)(2,1)} %bitcast.10), channel_id=1, source_target_pairs={{0,16},{16,0},{1,17},{17,1},{2,18},{18,2},{3,19},{19,3},{4,20},{20... | collective-permute-start | bytes 5308424 | tf_op jit(solution)/shard_map/ppermute | solution.py:31
  27.7 166.0 %all-gather.17.cloned.1.call-start = ((), (), s32[]{:S(2)}) async-start(), calls=%async_computation.12 | async-start | bytes 4423680 | tf_op jit(solution)/shard_map/all_gather | solution.py:1174
  28.7 11.3 collective-permute-start.2
  64.1 5.5 copy-start.17
  64.1 136.2 %all-gather.11.cloned.1.call-start = ((), (), s32[]{:S(2)}) async-start(), calls=%async_computation.5 | async-start | bytes 8847360 | tf_op jit(solution)/shard_map/all_gather | solution.py:1173
  64.9 211.9 %all-gather.19.cloned.1.call-start = ((), (), s32[]{:S(2)}) async-start(), calls=%async_computation.13 | async-start | bytes 2703360 | tf_op jit(solution)/shard_map/all_gather | solution.py:1207
  64.9 4.7 collective-permute-start.4
  200.3 197.6 %all-gather.21.cloned.1.call-start = ((), (), s32[]{:S(2)}) async-start(), calls=%async_computation.14 | async-start | bytes 4423680 | tf_op jit(solution)/shard_map/all_gather | solution.py:1209
  200.9 197.0 %all-gather.13.cloned.1.call-start = ((), (), s32[]{:S(2)}) async-start(), calls=%async_computation.6 | async-start | bytes 8847360 | tf_op jit(solution)/shard_map/all_gather | solution.py:1208
  201.5 656.9 %reduce-scatter.8.cloned.1.call-start = ((), (), s32[]{:S(2)}) async-start(), calls=%async_computation.7 | async-start | bytes 8847360 | tf_op jit(solution)/shard_map/reduce_scatter | solution.py:1260
  276.7 4.5 collective-permute-start.5
  488.1 90.2 %copy-start.30 = (bf16[1024,1536]{1,0:T(8,128)(2,1)S(1)}, bf16[1024,1536]{1,0:T(8,128)(2,1)}, u32[]{:S(2)}) copy-start(bf16[1024,1536]{1,0:T(8,128)(2,1)} %get-tuple-element.156) | copy-start | bytes 9437188
  578.2 10.6 copy-start.1
  588.7 19.7 %collective-permute-start.8 = (bf16[1536,2304]{1,0:T(8,128)(2,1)S(1)}, bf16[1536,2304]{1,0:T(8,128)(2,1)S(1)}, u32[]{:S(2)}, u32[]{:S(2)}) collective-permute-start(bf16[1536,2304]{1,0:T(8,128)(2,1)S(1)} %convolution_convert_fusion.4), channel_id=1, source_target_pairs={{0,16},{16,0},{1,17},{17,1},{2,18},{18,2},{3,19},{19,3},{4,20},{20... | collective-permute-start | bytes 21233672 | tf_op jit(solution)/shard_map/ppermute | solution.py:31
  599.4 6.4 collective-permute-start.9
  620.4 394.8 %reduce-scatter.10.cloned.1.call-start = ((), (), s32[]{:S(2)}) async-start(), calls=%async_computation.8 | async-start | bytes 4423680 | tf_op jit(solution)/shard_map/reduce_scatter | solution.py:1261
  722.4 92.4 %copy-start.28 = (bf16[1024,1536]{1,0:T(8,128)(2,1)S(1)}, bf16[1024,1536]{1,0:T(8,128)(2,1)}, u32[]{:S(2)}) copy-start(bf16[1024,1536]{1,0:T(8,128)(2,1)} %get-tuple-element.173) | copy-start | bytes 9437188
  826.6 20.5 %collective-permute-start.10 = (bf16[1536,2304]{1,0:T(8,128)(2,1)}, bf16[1536,2304]{1,0:T(8,128)(2,1)}, u32[]{:S(2)}, u32[]{:S(2)}) collective-permute-start(bf16[1536,2304]{1,0:T(8,128)(2,1)} %convolution_convert_fusion.1), channel_id=1, source_target_pairs={{0,16},{16,0},{1,17},{17,1},{2,18},{18,2},{3,19},{19,3},{4,20},{20... | collective-permute-start | bytes 21233672 | tf_op jit(solution)/shard_map/ppermute | solution.py:31
  826.6 194.2 %reduce-scatter.14.cloned.1.call-start = ((), (), s32[]{:S(2)}) async-start(), calls=%async_computation.10 | async-start | bytes 4423680 | tf_op jit(solution)/shard_map/reduce_scatter | solution.py:1261
  837.7 9.4 slice-start
  838.0 9.1 slice-start.1
  838.0 6.4 collective-permute-start.11
  858.5 162.4 %reduce-scatter.12.cloned.1.call-start = ((), (), s32[]{:S(2)}) async-start(), calls=%async_computation.9 | async-start | bytes 8847360 | tf_op jit(solution)/shard_map/reduce_scatter | solution.py:1260
  859.0 267.6 %reduce-scatter.16.cloned.1.call-start = ((), (), s32[]{:S(2)}) async-start(), calls=%async_computation.15 | async-start | bytes 4423680
  860.3 7.5 collective-permute-start.7
  873.5 131.3 %collective-permute-start.6 = (bf16[1024,1536]{1,0:T(8,128)(2,1)}, bf16[1024,1536]{1,0:T(8,128)(2,1)}, u32[]{:S(2)}, u32[]{:S(2)}) collective-permute-start(bf16[1024,1536]{1,0:T(8,128)(2,1)} %get-tuple-element.245), channel_id=1, source_target_pairs={{0,16},{1,17},{2,18},{3,19},{4,20},{5,21},{6,22},{7,23},{8,24},{9,... | collective-permute-start | bytes 9437192 | tf_op jit(solution)/shard_map/ppermute | solution.py:1234
  887.5 127.7 %collective-permute-start.13 = (bf16[1536,1152]{0,1:T(8,128)(2,1)}, bf16[1536,1152]{0,1:T(8,128)(2,1)}, u32[]{:S(2)}, u32[]{:S(2)}) collective-permute-start(bf16[1536,1152]{0,1:T(8,128)(2,1)} %fusion.5), channel_id=1, source_target_pairs={{0,16},{1,17},{2,18},{3,19},{4,20},{5,21},{6,22},{7,23},{8,24},{9,... | collective-permute-start | bytes 10616840 | tf_op jit(solution)/shard_map/ppermute | solution.py:1279
  1003.5 11.7 %collective-permute-start.12 = (bf16[1536,1152]{0,1:T(8,128)(2,1)}, bf16[1536,1152]{0,1:T(8,128)(2,1)}, u32[]{:S(2)}, u32[]{:S(2)}) collective-permute-start(bf16[1536,1152]{0,1:T(8,128)(2,1)} %fusion.4), channel_id=1, source_target_pairs={{16,0},{17,1},{18,2},{19,3},{20,4},{21,5},{22,6},{23,7},{24,8},{25... | collective-permute-start | bytes 10616840 | tf_op jit(solution)/shard_map/ppermute | solution.py:1278
  1006.8 94.3 %collective-permute-start.14 = (bf16[1024,1536]{1,0:T(8,128)(2,1)}, bf16[1024,1536]{1,0:T(8,128)(2,1)}, u32[]{:S(2)}, u32[]{:S(2)}) collective-permute-start(bf16[1024,1536]{1,0:T(8,128)(2,1)} %get-tuple-element.168.refs_11_), channel_id=1, source_target_pairs={{0,16},{1,17},{2,18},{3,19},{4,20},{5,21},{6,22},{7,23},{8,24},{9,... | collective-permute-start | bytes 9437192 | tf_op jit(solution)/shard_map/ppermute | solution.py:1234
  1026.4 5.2 copy-start.22
  1026.5 7.8 copy-start.24
  1032.3 63.6 %collective-permute-start.21 = (f32[2,1536]{1,0:T(2,128)}, f32[2,1536]{1,0:T(2,128)}, u32[]{:S(2)}, u32[]{:S(2)}) collective-permute-start(f32[2,1536]{1,0:T(2,128)} %pad_maximum_fusion.12), channel_id=1, source_target_pairs={{0,16},{1,17},{2,18},{3,19},{4,20},{5,21},{6,22},{7,23},{8,24},{9,... | collective-permute-start | bytes 36872 | tf_op jit(solution)/shard_map/ppermute | solution.py:1291
  1034.8 63.4 %copy-start.11 = (bf16[384,2304]{1,0:T(8,128)(2,1)S(1)}, bf16[384,2304]{1,0:T(8,128)(2,1)}, u32[]{:S(2)}) copy-start(bf16[384,2304]{1,0:T(8,128)(2,1)} %reduce-scatter.12.cloned.1.call-done) | copy-start | bytes 5308420
  1088.9 9.3 copy-start.10
  1091.9 4.0 collective-permute-start.20
  1094.7 11.0 collective-permute-start.19
  1096.6 4.2 collective-permute-start.22
  1099.6 9.5 collective-permute-start.18
  1099.6 23.1 %collective-permute-start.15 = (bf16[1024,1536]{1,0:T(8,128)(2,1)}, bf16[1024,1536]{1,0:T(8,128)(2,1)}, u32[]{:S(2)}, u32[]{:S(2)}) collective-permute-start(bf16[1024,1536]{1,0:T(8,128)(2,1)} %get-tuple-element.194), channel_id=1, source_target_pairs={{16,0},{17,1},{18,2},{19,3},{20,4},{21,5},{22,6},{23,7},{24,8},{25... | collective-permute-start | bytes 9437192 | tf_op jit(solution)/shard_map/ppermute | solution.py:1233
  1100.9 4.2 collective-permute-start.23
  1122.7 8.2 copy-start.6
  1130.8 7.3 collective-permute-start.16
  1130.8 5.3 copy-start.14
  1138.1 15.3 %collective-permute-start.17 = (bf16[400,256]{0,1:T(8,128)(2,1)S(1)}, bf16[400,256]{0,1:T(8,128)(2,1)S(1)}, u32[]{:S(2)}, u32[]{:S(2)}) collective-permute-start(bf16[400,256]{0,1:T(8,128)(2,1)S(1)} %add_convert_fusion.3), channel_id=1, source_target_pairs={{0,2},{2,0},{1,3},{3,1},{4,6},{6,4},{5,7},{7,5},{8,10},{10,8},{9,1... | collective-permute-start | bytes 614408 | tf_op jit(solution)/shard_map/ppermute | solution.py:1311
  (20 other events, 62.2 us)
Sparse Core Ops, SparseCore 0:
  27.8 36.2 all-gather.14
  66.0 56.0 all-gather.16
  124.5 75.7 all-gather.10
  202.6 35.8 all-gather.18
  240.1 47.2 all-gather.20
  289.7 87.4 all-gather.12
  620.5 86.4 reduce-scatter.7
  826.8 46.5 reduce-scatter.9
  876.5 48.7 reduce-scatter.13
  928.2 81.4 reduce-scatter.11
  1024.7 46.2 reduce-scatter.15
where the time goes:
time: 1170 us; the launch traced here: 1160 us
  Pallas kernels  823 us (70%)
  other arithmetic  80 us (7%)
  matrix products  78.3 us (7%)
  local copies, waits for them, and re-layouts  71.2 us (6%)
  waiting for transfers between devices  64.2 us (5%)
  starting transfers between devices  31.9 us (3%)
  between operations  15.3 us (1%)
    pallas_call x2, Pallas kernels, attention_forward(): pl.pallas_call(functools.partial(attention_forward_kernel, low), out_shap...  216 us
    pallas_call x2, Pallas kernels, attention_backward(): pl.pallas_call(attention_backward_kernel, out_shape=outs, in_specs=[VMEM]...  205 us
    pallas_call x2, Pallas kernels, ffn_backward(): pl.pallas_call(functools.partial(ffn_backward_kernel, low), out_shape=[wi...  183 us
    pallas_call x2, Pallas kernels, ffn_forward(): pl.pallas_call(functools.partial(ffn_forward_kernel, lead), out_shape=[bo...  165 us
    dot_general x10, matrix products, dot(): return jnp.einsum(form, left, right, preferred_element_type=F32)  78.3 us
    pallas_call x1, Pallas kernels, last_grads(): pl.pallas_call(last_kernel, out_shape=[jax.ShapeDtypeStruct(grad.shape, B...  54.1 us
    unnamed x87, local copies, waits for them, and re-layouts  31.1 us
  transfers between devices with their start and end apart: 35, of which 10 were waited for; matrix products, arithmetic and copies ran while one was open for 16% of the time, Pallas kernels for 55%

commit v1 on v0

--- a/solution.py
+++ b/solution.py
@@ -643,6 +643,51 @@
     return (key_at <= row_at) & (own == seg_keys[...])
 
 
+class AttentionWeights:
+    def __init__(self, sources, targets, sems):
+        self.own, self.other = sources
+        self.w_lin, self.w_out = targets
+        self.sems = sems
+
+    def copies(self):
+        sec = lax.axis_index("section")
+        q_cols = self.w_out.shape[1]
+        heads_here = q_cols // HEAD
+        head = lax.axis_index("tp") * heads_here // (HEADS // KV_HEADS)
+        shards, half = self.own.shape[:2]
+        for k, (source, side) in enumerate(((self.own, sec), (self.other, 1 - sec))):
+            for i in range(shards):
+                rows = pl.ds(pl.multiple_of((2 * i + side) * half, 16), half)
+                key_at = pl.multiple_of(q_cols + head * HEAD, HEAD)
+                value_at = pl.multiple_of(q_cols + (KV_HEADS + head) * HEAD, HEAD)
+                pieces = (
+                    (pl.ds(0, q_cols), self.w_lin.at[rows, pl.ds(0, q_cols)]),
+                    (pl.ds(key_at, HEAD), self.w_lin.at[rows, pl.ds(q_cols, HEAD)]),
+                    (pl.ds(value_at, HEAD), self.w_lin.at[rows, pl.ds(q_cols + HEAD, HEAD)]),
+                    (pl.ds(q_cols + 2 * KV_HEADS * HEAD, q_cols), self.w_out.at[rows]),
+                )
+                for p, (columns, target) in enumerate(pieces):
+                    yield pltpu.make_async_copy(source.at[i, :, columns], target, self.sems.at[k, i, p])
+
+    def start(self):
+        for copy in self.copies():
+            copy.start()
+
+    def wait(self):
+        for copy in self.copies():
+            copy.wait()
+
+
+def attention_scratch(halves, q_cols):
+    shards, half = halves[0].shape[:2]
+    width = 2 * shards * half
+    return [
+        pltpu.VMEM((width, q_cols + 2 * HEAD), BF16),
+        pltpu.VMEM((width, q_cols), BF16),
+        pltpu.SemaphoreType.DMA((2, shards, 4)),
+    ]
+
+
 def attention_forward_stage(layer_in, gain, w_lin, w_out, bias, places, outs, result, kv_sems, tick):
     cosine, sine, seg_rows, seg_keys = places
     normed, query, kv, lse, attended = outs
@@ -710,7 +755,8 @@
 
 def attention_forward_kernel(low, *refs):
     take = Taker(refs)
-    gain, w_lin, w_out, bias = take(4)
+    gain, bias = take(2)
+    halves = take(2)
     places_a, places_b = take(4), take(4)
     layer_a, layer_b = ab(take(1)[0])
     if not low:
@@ -722,6 +768,9 @@
         result_b, total_a, last_sum_b, layer = take(4)
         layer_a, layer_b = ab(layer)
     result_a, kv_sems_a, kv_sems_b = take(3)
+    w_lin, w_out, w_sems = take(3)
+    weights = AttentionWeights(halves, (w_lin, w_out), w_sems)
+    weights.start()
     if low:
         (result_b,) = take(1)
     chain_a = Chain(result_a, total_a, *take(CHAIN_REFS))
@@ -734,6 +783,7 @@
             layer_a[rows] = sum(ref[rows].astype(F32) for ref in adds_a).astype(BF16)
 
         by_rows(layer_a.shape[0], body)
+    weights.wait()
     tick = ticker(None if low else chain_b, 0)
     done = attention_forward_stage(layer_a, gain, w_lin, w_out, bias, places_a, outs_a, result_a, kv_sems_a, tick)
     chain_a.start()
@@ -758,9 +808,8 @@
 
 
 def attention_forward(weights, places, inputs):
-    w_lin, w_out, gains, bias = weights
+    halves, q_cols, gains, bias = weights
     rows, width = inputs[0].shape[0] // 2, inputs[0].shape[1]
-    q_cols = w_out.shape[1]
     keys = places[0][3].shape[1]
     count = keys // rows
     low = len(inputs) == 1
@@ -769,14 +818,15 @@
     kv_out = jax.ShapeDtypeStruct((2 * keys, 2 * HEAD), BF16)
     lse_out = jax.ShapeDtypeStruct((2 * rows, HEAD), F32)
     outs = [both, heads_out, kv_out, lse_out, heads_out] + ([narrow] * 2 if low else [narrow] * 3 + [both])
-    args = (gains[:1], w_lin, w_out, bias, *places[0], *places[1], *inputs)
+    args = (gains[:1], bias, *halves, *places[0], *places[1], *inputs)
     return pl.pallas_call(
         functools.partial(attention_forward_kernel, low),
         out_shape=outs,
-        in_specs=[VMEM] * len(args),
+        in_specs=[VMEM] * 2 + [ANY] * 2 + [VMEM] * (len(args) - 4),
         out_specs=[VMEM] * len(outs),
         scratch_shapes=[pltpu.VMEM((rows, width), BF16)]
         + [pltpu.SemaphoreType.DMA((2, count))] * 2
+        + attention_scratch(halves, q_cols)
         + [pltpu.VMEM((rows, width), BF16)] * low
         + chain_scratch((rows, width)) * 2,
         compiler_params=params(5 + low),
@@ -863,7 +913,8 @@
 
 def attention_backward_kernel(*refs):
     take = Taker(refs)
-    gain, w_lin, w_out = take(3)
+    (gain,) = take(1)
+    halves = take(2)
     places_a, places_b = take(4), take(4)
     ins_a, ins_b = zip(*[ab(ref) for ref in take(6)])
     attn_a, attn_b = take(2)
@@ -872,12 +923,16 @@
     outs_a, outs_b = zip(*[ab(ref) for ref in take(2)])
     gain_grad, result_b, total_a, total_b = take(4)
     heads_grad, kv_grad, q_part, result_a = take(4)
+    w_lin, w_out, w_sems = take(3)
+    weights = AttentionWeights(halves, (w_lin, w_out), w_sems)
+    weights.start()
     exchange_a, exchange_b = take(3), take(3)
     chain_a = Chain(result_a, total_a, *take(CHAIN_REFS))
     chain_b = Chain(last_b, total_b, *take(CHAIN_REFS))
     greet(exchange_a[2].shape[1])
     chain_b.start()
     gain_grad[...] = jnp.zeros_like(gain_grad)
+    weights.wait()
     scratch = (heads_grad, kv_grad, q_part, *exchange_a)
     done = attention_backward_stage(
         ins_a, sum_a, gain, w_lin, w_out, places_a, outs_a, gain_grad, result_a, scratch, ticker(chain_b, 0)
@@ -895,9 +950,8 @@
 
 
 def attention_backward(upstream, sum_a, last_b, kept, weights, places):
-    w_lin, w_out, gains, bias = weights
+    halves, q_cols, gains, bias = weights
     rows, width = sum_a.shape
-    q_cols = w_out.shape[1]
     keys = places[0][3].shape[1]
     count = keys // rows
     narrow = jax.ShapeDtypeStruct((rows, width), BF16)
@@ -905,13 +959,13 @@
     lin_out = jax.ShapeDtypeStruct((2 * rows, q_cols + 2 * HEAD), BF16)
     outs = [both, lin_out] + [jax.ShapeDtypeStruct((8, width), F32)] + [narrow] * 3
     names = ("layer_in", "query", "kv", "lse", "attended", "attn_a", "attn_b")
-    args = (gains[1:], w_lin, w_out, *places[0], *places[1], upstream)
+    args = (gains[1:], *halves, *places[0], *places[1], upstream)
     args += (*[kept[name] for name in names], sum_a, last_b)
     exchange = [pltpu.VMEM((max(count - 1, 1), rows, 2 * HEAD), BF16)] * 2 + [pltpu.SemaphoreType.DMA((2, count))]
     return pl.pallas_call(
         attention_backward_kernel,
         out_shape=outs,
-        in_specs=[VMEM] * len(args),
+        in_specs=[VMEM] + [ANY] * 2 + [VMEM] * (len(args) - 3),
         out_specs=[VMEM] * len(outs),
         scratch_shapes=[
             pltpu.VMEM((rows, q_cols), BF16),
@@ -919,6 +973,7 @@
             pltpu.VMEM((rows, width), F32),
             pltpu.VMEM((rows, width), BF16),
         ]
+        + attention_scratch(halves, q_cols)
         + exchange * 2
         + chain_scratch((rows, width)) * 2,
         compiler_params=params(7),
@@ -934,12 +989,29 @@
     return (jnp.cos(angles), jnp.sin(angles))
 
 
+def norm_back(grad_out, rows_in, factor, gain):
+    unit = rows_in * factor
+    gain_grad = jnp.sum(grad_out * unit, axis=0)
+    weighted = grad_out * gain
+    return (
+        factor * (weighted - unit * jnp.mean(weighted * unit, axis=-1, keepdims=True)),
+        gain_grad,
+    )
+
+
 def over_ctx(value):
     if lax.axis_size("ctx") == 2:
         other = lax.ppermute(value, "ctx", [(0, 1), (1, 0)])
         low = lax.axis_index("ctx") == 0
         return jnp.concatenate([jnp.where(low, value, other), jnp.where(low, other, value)], axis=-1)
     return lax.all_gather(value, "ctx", axis=value.ndim - 1, tiled=True)
+
+
+def input_backward(normed_one_grad, middle_grad, kept, gains):
+    layer_in = kept["layer_in"].astype(F32)
+    factor = lax.rsqrt(jnp.mean(layer_in * layer_in, axis=-1, keepdims=True) + EPS)
+    norm_grad, gain_one = norm_back(normed_one_grad.astype(F32), layer_in, factor, gains[0])
+    return (middle_grad.astype(F32) + norm_grad).astype(BF16), gain_one
 
 
 def local(
@@ -978,9 +1050,6 @@
         mine = lax.dynamic_slice_in_dim(rows, sec * half, half, 0)
         return per_layer(mine, swap(lax.dynamic_slice_in_dim(rows, (1 - sec) * half, half, 0)))
 
-    def joined(own):
-        return jnp.stack(per_layer(own, swap(own)), axis=1).reshape(width, own.shape[-1])
-
     def after(value, event):
         return lax.optimization_barrier((value, event))[0]
 
@@ -1023,12 +1092,9 @@
     down_low = lax.all_gather(down_shards[0], ranks, axis=0)
 
     def attention_weights(own):
-        p = joined(own)
-        wq = p[:, :q_cols]
-        wk = lax.dynamic_slice_in_dim(p[:, q_cols : q_cols + kv_width], head_pick * HEAD, HEAD, 1)
-        wv = lax.dynamic_slice_in_dim(p[:, q_cols + kv_width : q_cols + 2 * kv_width], head_pick * HEAD, HEAD, 1)
-        wo = p[:, q_cols + 2 * kv_width : 2 * q_cols + 2 * kv_width]
-        s = p[:, 2 * q_cols + 2 * kv_width :]
+        parts = own, swap(own)
+        small = [part[..., 2 * q_cols + 2 * kv_width :] for part in parts]
+        s = jnp.stack(per_layer(*small), axis=1).reshape(width, -1)
         gains = s[:, :2].T
         s = s[:, 2:n_extra].T.reshape(-1, shards, shard).transpose(1, 0, 2).reshape(shards, -1)[:, :n_biases]
         q_b = s[:, : heads_here * piece].reshape(shards, heads_here, piece).transpose(1, 0, 2).reshape(heads_here, HEAD)
@@ -1036,160 +1102,8 @@
         kv_b = kv_b.transpose(1, 2, 0, 3).reshape(2, KV_HEADS, HEAD)
         kv_b = lax.dynamic_slice_in_dim(kv_b, head_pick, 1, 1)
         bias = jnp.concatenate([q_b.reshape(1, -1), kv_b.reshape(1, -1)], axis=1).astype(F32)
-        return jnp.concatenate([wq, wk, wv], axis=1), wo, gains.astype(F32), bias
-
-    names = ("layer_in", "query", "kv", "lse", "attended", "attn_a", "attn_b")
-    args = (gains[1:], w_lin, w_out, *places[0], *places[1], upstream)
-    args += (*[kept[name] for name in names], sum_a, last_b)
-    exchange = [pltpu.VMEM((max(count - 1, 1), rows, 2 * HEAD), BF16)] * 2 + [pltpu.SemaphoreType.DMA((2, count))]
-    return pl.pallas_call(
-        attention_backward_kernel,
-        out_shape=outs,
-        in_specs=[VMEM] * len(args),
-        out_specs=[VMEM] * len(outs),
-        scratch_shapes=[
-            pltpu.VMEM((rows, q_cols), BF16),
-            pltpu.VMEM((keys, 2 * HEAD), F32),
-            pltpu.VMEM((rows, width), F32),
-            pltpu.VMEM((rows, width), BF16),
-        ]
-        + exchange * 2
-        + chain_scratch((rows, width)) * 2,
-        compiler_params=params(7),
-        cost_estimate=cost(),
-    )(*args)
-
-
-def rope_tables(places):
-    steps = jnp.arange(HEAD // 2, dtype=F32) * (2.0 / HEAD)
-    inverse = ROPE_BASE ** (-steps)
-    angles = places.astype(F32)[..., None] * inverse
-    angles = jnp.concatenate([angles, angles], axis=-1)
-    return (jnp.cos(angles), jnp.sin(angles))
-
-
-def norm_back(grad_out, rows_in, factor, gain):
-    unit = rows_in * factor
-    gain_grad = jnp.sum(grad_out * unit, axis=0)
-    weighted = grad_out * gain
-    return (
-        factor * (weighted - unit * jnp.mean(weighted * unit, axis=-1, keepdims=True)),
-        gain_grad,
-    )
-
-
-def over_ctx(value):
-    if lax.axis_size("ctx") == 2:
-        other = lax.ppermute(value, "ctx", [(0, 1), (1, 0)])
-        low = lax.axis_index("ctx") == 0
-        return jnp.concatenate([jnp.where(low, value, other), jnp.where(low, other, value)], axis=-1)
-    return lax.all_gather(value, "ctx", axis=value.ndim - 1, tiled=True)
-
-
-def input_backward(normed_one_grad, middle_grad, kept, gains):
-    layer_in = kept["layer_in"].astype(F32)
-    factor = lax.rsqrt(jnp.mean(layer_in * layer_in, axis=-1, keepdims=True) + EPS)
-    norm_grad, gain_one = norm_back(normed_one_grad.astype(F32), layer_in, factor, gains[0])
-    return (middle_grad.astype(F32) + norm_grad).astype(BF16), gain_one
-
-
-def local(
-    section_in,
-    segments,
-    positions,
-    query_weight,
-    kv_weight,
-    output_weight,
-    gate_up,
-    down_weight,
-    norm_gains,
-    query_bias,
-    kv_bias,
-    out_grad,
-):
-    sec = lax.axis_index("section")
-    first = sec == 0
-    group = HEADS // KV_HEADS
-    heads_here = HEADS // lax.axis_size("tp")
-    head_pick = lax.axis_index("tp") * heads_here // group
-    shards = lax.axis_size("dp") * lax.axis_size("ctx")
-    ranks = ("dp", "ctx")
-    seqs, span, width = section_in.shape[1:]
-    shard = query_weight.shape[1]
-    q_cols = query_weight.shape[2]
-    ff = gate_up.shape[3]
-
-    def per_layer(mine, theirs):
-        return jnp.where(first, mine, theirs), jnp.where(first, theirs, mine)
-
-    half = shard // 2
-    kv_width = KV_HEADS * HEAD
-
-    def halves(rows):
-        mine = lax.dynamic_slice_in_dim(rows, sec * half, half, 0)
-        return per_layer(mine, swap(lax.dynamic_slice_in_dim(rows, (1 - sec) * half, half, 0)))
-
-    def joined(own):
-        return jnp.stack(per_layer(own, swap(own)), axis=1).reshape(width, own.shape[-1])
-
-    def after(value, event):
-        return lax.optimization_barrier((value, event))[0]
-
-    piece = HEAD // shards
-    biases = jnp.concatenate([query_bias[0].reshape(-1), kv_bias[0].reshape(-1)])
-    n_biases = biases.shape[0]
-    biases = jnp.pad(biases, (0, -n_biases % shard)).reshape(-1, shard).T
-    extra = jnp.concatenate([norm_gains[0].T, biases], axis=1)
-    n_extra = extra.shape[1]
-    extra = jnp.pad(extra, ((0, 0), (0, HEAD - n_extra)))
-    packed = jnp.concatenate([query_weight[0], kv_weight[0, 0], kv_weight[0, 1], output_weight[0].T, extra], axis=1)
-    packed_shards = halves(packed)
-    first_shard, gate_up, down_weight, positions, segments, section_in = lax.optimization_barrier(
-        (packed_shards[0], gate_up, down_weight, positions, segments, section_in)
-    )
-    packed_low = lax.all_gather(first_shard, ranks, axis=0)
-    spare = -ff % TILE
-    wide = jnp.pad(gate_up[0], ((0, 0), (0, 0), (0, spare)))
-    mine = lax.dynamic_index_in_dim(wide, sec, 0, keepdims=False)
-    theirs = swap(lax.dynamic_index_in_dim(wide, 1 - sec, 0, keepdims=False))
-    gate_up_shards = per_layer(mine, theirs)
-    down_shards = halves(jnp.pad(down_weight[0].T, ((0, 0), (0, spare))))
-
-    micro = sec
-    seg = lax.dynamic_index_in_dim(segments, micro, 0, keepdims=False)
-    pos = lax.dynamic_index_in_dim(positions, micro, 0, keepdims=False)
-    hidden = lax.dynamic_index_in_dim(section_in, micro, 0, keepdims=False)
-    seg_keys = over_ctx(seg)
-    segs, tables = [], []
-    for q in range(seqs):
-        segs.append((seg[q][:, None], seg_keys[q][None]))
-        cosine, sine = rope_tables(pos[q])
-        tables.append((cosine, jnp.where(jnp.arange(HEAD) < HEAD // 2, -sine, sine)))
-    hidden = hidden.reshape(seqs * span, width)
-
-    packed_low, gate_up_shards, down_shards, packed_shards, segs, tables, hidden = lax.optimization_barrier(
-        (packed_low, gate_up_shards, down_shards, packed_shards, segs, tables, hidden)
-    )
-    own_low = lax.all_gather(gate_up_shards[0], ranks, axis=0, tiled=True)
-    down_low = lax.all_gather(down_shards[0], ranks, axis=0)
-
-    def attention_weights(own):
-        p = joined(own)
-        wq = p[:, :q_cols]
-        wk = lax.dynamic_slice_in_dim(p[:, q_cols : q_cols + kv_width], head_pick * HEAD, HEAD, 1)
-        wv = lax.dynamic_slice_in_dim(p[:, q_cols + kv_width : q_cols + 2 * kv_width], head_pick * HEAD, HEAD, 1)
-        wo = p[:, q_cols + 2 * kv_width : 2 * q_cols + 2 * kv_width]
-        s = p[:, 2 * q_cols + 2 * kv_width :]
-        gains = s[:, :2].T
-        s = s[:, 2:n_extra].T.reshape(-1, shards, shard).transpose(1, 0, 2).reshape(shards, -1)[:, :n_biases]
-        q_b = s[:, : heads_here * piece].reshape(shards, heads_here, piece).transpose(1, 0, 2).reshape(heads_here, HEAD)
-        kv_b = s[:, heads_here * piece :].reshape(shards, 2, KV_HEADS, piece)
-        kv_b = kv_b.transpose(1, 2, 0, 3).reshape(2, KV_HEADS, HEAD)
-        kv_b = lax.dynamic_slice_in_dim(kv_b, head_pick, 1, 1)
-        bias = jnp.concatenate([q_b.reshape(1, -1), kv_b.reshape(1, -1)], axis=1).astype(F32)
-        return jnp.concatenate([wq, wk, wv], axis=1), wo, gains.astype(F32), bias
-
-    kept = [[dict(), dict()] for _ in range(2)]
+        return parts, q_cols, gains.astype(F32), bias
+
     names = ("normed", "query", "kv", "lse", "attended")
     more_names = ("normed_two", "gate", "up", "inner")
     attn_weights, ffn_weights = [attention_weights(packed_low), None], [None, None]
@@ -1229,13 +1143,17 @@
     attn_sum, ffn_sum = jnp.concatenate([attn_a, attn_b]), jnp.concatenate([ffn_a, ffn_b])
     outs = [layer_in, (layer_in.astype(F32) + attn_sum.astype(F32) + ffn_sum.astype(F32)).astype(BF16)]
 
-    def to_section(values):
-        low = lax.ppermute(values[0], "section", [(1, 0)])
-        high = lax.ppermute(values[1], "section", [(0, 1)])
+    def to_section(values, low, high):
         both = jnp.stack([jnp.where(first, values[0], high), jnp.where(first, low, values[1])])
         return both.reshape(2, seqs, span, width)
 
-    section_out = to_section(outs)
+    def to_low(value):
+        return lax.ppermute(value, "section", [(1, 0)])
+
+    def to_high(value):
+        return lax.ppermute(value, "section", [(0, 1)])
+
+    out_low, out_high = to_low(outs[0]), to_high(outs[1])
 
     in_grads = [None, None]
     gate_up_grads, down_grads, packed_grads, gains_grads = [[None, None] for _ in range(4)]
@@ -1247,15 +1165,18 @@
                 attn_grad, k["gate"], k["up"], ffn_weights[0], part_b, below
             )
             in_grads[1] = upstream
+            in_high = to_high(upstream)
             gains_grads[1] = jnp.stack([jnp.sum(gain_one, axis=0), gain_two])
             sum_a, gate_up_grads[1] = lax.optimization_barrier((sum_a, gate_up_grads[1]))
         own_w, other_w = [dot("rd,rf->df", k["normed_two"], g).astype(BF16) for g in wide_grads]
-        own_w = (own_w.astype(F32) + swap(other_w).astype(F32)).astype(BF16)
+        other_w = swap(other_w)
         down_w = dot("rd,rf->df", upstream, k["inner"]).astype(BF16)
         down_w = down_w.reshape(shards, 2, half, ff + spare)
         down_own = lax.dynamic_index_in_dim(down_w, sec, 1, keepdims=False)
-        down_other = lax.dynamic_index_in_dim(down_w, 1 - sec, 1, keepdims=False)
-        down_own = (down_own.astype(F32) + swap(down_other).astype(F32)).astype(BF16)
+        down_other = swap(lax.dynamic_index_in_dim(down_w, 1 - sec, 1, keepdims=False))
+        own_w = (own_w.astype(F32) + other_w.astype(F32)).astype(BF16)
+        own_w, down_other = lax.optimization_barrier((own_w, down_other))
+        down_own = (down_own.astype(F32) + down_other.astype(F32)).astype(BF16)
         own_w, down_own, sum_a = lax.optimization_barrier((own_w, down_own, sum_a))
         gate_up_grads[layer] = lax.psum_scatter(own_w, ranks, scatter_dimension=0, tiled=True)
         down_grads[layer] = lax.psum_scatter(
@@ -1265,7 +1186,9 @@
         attn_grad, lin_grad, gain_two, part_b, sum_a, _ = attention_backward(upstream, sum_a, grad_b, k, weights, places)
         gain_two = jnp.sum(gain_two, axis=0)
         if layer == 0:
-            part_b, down_grads[1] = lax.optimization_barrier((part_b, down_grads[1]))
+            part_b, down_grads[1], out_low, out_high, in_high = lax.optimization_barrier(
+                (part_b, down_grads[1], out_low, out_high, in_high)
+            )
         lin_w = dot("rd,re->de", k["normed"], lin_grad)
         out_w = dot("rd,re->de", attn_grad, k["attended"])
         bias = jnp.sum(lin_grad.astype(F32), axis=0)
@@ -1286,7 +1209,7 @@
     packed_total = lax.psum_scatter(packed_total, ranks, scatter_dimension=0, tiled=True).astype(F32)
     in_grads[0], gain_one = last_grads(last_part, sum_a, attn_grad, kept[0]["layer_in"], attn_weights[0][2][:1])
     gains_grads[0] = jnp.stack([jnp.sum(gain_one, axis=0), gain_two])
-    input_grad = to_section(in_grads)
+    in_low = to_low(in_grads[0])
     low = lax.ppermute(gains_grads[0], "section", [(1, 0)])
     high = lax.ppermute(gains_grads[1], "section", [(0, 1)])
     gains_grad = jnp.where(first, gains_grads[0] + low, gains_grads[1] + high)
@@ -1307,6 +1230,7 @@
     kv_bias = bias[heads_here:].reshape(1, -1)
     kv_bias = jnp.pad(kv_bias, ((0, 15), (0, -kv_bias.shape[1] % (2 * HEAD))))
     mine = jnp.concatenate([kv_narrow.reshape(shard, 2 * HEAD), kv_bias[:, : 2 * HEAD]]).astype(BF16)
+    mine, gate_up_grads, down_grads = lax.optimization_barrier((mine, gate_up_grads, down_grads))
     mine = (mine.astype(F32) + lax.ppermute(mine, "tp", [(0, 1), (1, 0), (2, 3), (3, 2)]).astype(F32)).astype(BF16)
     theirs = lax.ppermute(mine, "tp", [(0, 2), (2, 0), (1, 3), (3, 1)])
     mine, theirs = mine.astype(F32), theirs.astype(F32)
@@ -1320,6 +1244,8 @@
         other = swap(jnp.where(first, values[1], values[0]))
         return jnp.where(first, kept_half, other), jnp.where(first, other, kept_half)
 
+    section_out = to_section(outs, out_low, out_high)
+    input_grad = to_section(in_grads, in_low, in_high)
     gate_up_grad = jnp.stack(collect(gate_up_grads))[..., :ff].astype(F32)
     down_grad = jnp.concatenate(collect(down_grads), axis=0)[:, :ff].T.astype(F32)
     return (

time: 1170 us -> 1170 us (level)
    ppermute x11, waiting for transfers between devices: 16.5 us -> 4.82 us  [swap(): return lax.ppermute(value, 'section', [(0, 1), (1, 0)])]
    unnamed x87 -> x105, local copies, waits for them, and re-layouts: 31.1 us -> 39.1 us
  transfers between devices with their start and end apart: 35 -> 35, of which waited for: 10 -> 11; matrix products, arithmetic and copies ran while one was open for 16% -> 14% of each run, Pallas kernels for 55% -> 56%
where the time goes in v1:
time: 1170 us; the launch traced here: 1160 us
  Pallas kernels  830 us (71%)
  matrix products  79.9 us (7%)
  local copies, waits for them, and re-layouts  73.9 us (6%)
  other arithmetic  72.9 us (6%)
  waiting for transfers between devices  58.5 us (5%)
  starting transfers between devices  33.4 us (3%)
  between operations  15.1 us (1%)
    pallas_call x2, Pallas kernels, attention_forward(): pl.pallas_call(functools.partial(attention_forward_kernel, low), out_shap...  218 us
    pallas_call x2, Pallas kernels, attention_backward(): pl.pallas_call(attention_backward_kernel, out_shape=outs, in_specs=[VMEM]...  210 us
    pallas_call x2, Pallas kernels, ffn_backward(): pl.pallas_call(functools.partial(ffn_backward_kernel, low), out_shape=[wi...  183 us
    pallas_call x2, Pallas kernels, ffn_forward(): pl.pallas_call(functools.partial(ffn_forward_kernel, lead), out_shape=[bo...  165 us
    dot_general x10, matrix products, dot(): return jnp.einsum(form, left, right, preferred_element_type=F32)  79.9 us
    pallas_call x1, Pallas kernels, last_grads(): pl.pallas_call(last_kernel, out_shape=[jax.ShapeDtypeStruct(grad.shape, B...  54.1 us
    unnamed x105, local copies, waits for them, and re-layouts  39.1 us
  transfers between devices with their start and end apart: 35, of which 11 were waited for; matrix products, arithmetic and copies ran while one was open for 14% of the time, Pallas kernels for 56%

profile of v1, /device:TPU:0, one launch (start us, length us, event | category | flops | bytes accessed | tf_op | source)
XLA Modules:
  0.0 1163.5 jit_solution(15069102475370691668)
XLA Ops:
  17.8 2.9 collective-permute-start.3
  20.7 3.5 pad_dynamic-slice_fusion.1
  24.2 2.3 copy.182
  29.4 2.8 negate_select_fusion
  32.3 3.8 constant_dynamic-slice_fusion.8
  36.0 2.7 copy.181
  40.0 2.7 broadcast_select_fusion.10
  42.7 3.5 bitcast_select_fusion
  46.2 17.9 %all-gather.15.cloned.1.call-done = bf16[768,1408]{1,0:T(8,128)(2,1)} async-done(((bf16[192,1408]{1,0:T(8,128)(2,1)}), bf16[768,1408]{1,0:T(8,128)(2,1)}) %all-gather.15.cloned.1.call-update) | async-done | bytes 2162704 | tf_op jit(solution)/shard_map/all_gather | solution.py:1068
  66.8 2.7 collective-permute-done.4.refs_3_.refs_2_
  73.0 117.6 %shard_map.195 = (bf16[1024,1536]{1,0:T(8,128)(2,1)}, bf16[1024,384]{1,0:T(8,128)(2,1)}, bf16[2048,256]{1,0:T(8,128)(2,1)}, f32[1024,128]{1,0:T(8,128)}, bf16[10...) custom-call(f32[1,1536]{1,0:T(1,128)} %get-tuple-element.314.refs_0_.gain, ...), custom_call_target="tpu_custom_call" | custom-call | flops 1048576 | bytes 1048576 | tf_op jit(solution)/shard_map/pallas_call | solution.py:822
  190.6 12.5 %all-gather.11.cloned.1.call-done.refs_4_ = bf16[1536,2304]{1,0:T(8,128)(2,1)} async-done(((bf16[384,2304]{1,0:T(8,128)(2,1)}), bf16[1536,2304]{1,0:T(8,128)(2,1)}) %all-gather.11.cloned.1.call-update) | async-done | bytes 7077904 | tf_op jit(solution)/shard_map/all_gather | solution.py:1091
  204.4 75.2 %shard_map.196 = (bf16[1024,1536]{1,0:T(8,128)(2,1)}, bf16[1024,2304]{1,0:T(8,128)(2,1)}, bf16[1024,2304]{1,0:T(8,128)(2,1)}, bf16[1024,2304]{1,0:T(8,128)(2,1)}...) custom-call(bf16[1024,1536]{1,0:T(8,128)(2,1)} %bitcast.159, ...), custom_call_target="tpu_custom_call" | custom-call | flops 1048576 | bytes 1048576 | tf_op jit(solution)/shard_map/pallas_call | solution.py:458
  279.8 3.8 constant_dynamic-slice_fusion.5
  287.7 100.4 %shard_map.197 = (bf16[1024,1536]{1,0:T(8,128)(2,1)}, bf16[1024,384]{1,0:T(8,128)(2,1)}, bf16[2048,256]{1,0:T(8,128)(2,1)}, f32[1024,128]{1,0:T(8,128)}, bf16[10...) custom-call(f32[1,1536]{1,0:T(1,128)} %get-tuple-element.312.refs_0_, ...), custom_call_target="tpu_custom_call" | custom-call | flops 1048576 | bytes 1048576 | tf_op jit(solution)/shard_map/pallas_call | solution.py:822
  388.1 90.1 %shard_map.198 = (bf16[1024,1536]{1,0:T(8,128)(2,1)}, bf16[1024,2304]{1,0:T(8,128)(2,1)}, bf16[1024,2304]{1,0:T(8,128)(2,1)}, bf16[1024,2304]{1,0:T(8,128)(2,1)}...) custom-call(bf16[1024,1536]{1,0:T(8,128)(2,1)} %get-tuple-element.148.refs_0_.refs_12_.refs_7_, ...), custom_call_target="tpu_custom_call" | custom-call | flops 1048576 | bytes 1048576 | tf_op jit(solution)/shard_map/pallas_call | solution.py:458
  478.3 90.2 %shard_map.199 = (bf16[1024,2304]{1,0:T(8,128)(2,1)}, bf16[1024,2304]{1,0:T(8,128)(2,1)}, bf16[512,1536]{1,0:T(8,128)(2,1)}, bf16[512,1536]{1,0:T(8,128)(2,1)}, bf16[512,1536]{1,0:T(8,128)(2,1)}) custom-call(bf16[1024,1536]{1,0:T(8,128)(2,1)} %bitcast.163, bf16[512,1536]{1,0:T(8,128)(2,1)} %get-tuple-element.164.refs_1_, ...), custom_call_target="tpu_custom_call" | custom-call | flops 1048576 | bytes 1048576 | tf_op jit(solution)/shard_map/pallas_call | solution.py:586
  568.5 10.5 convolution_convert_fusion.4
  579.1 10.4 convolution_convert_fusion.3
  589.7 2.6 copy-done.13
  592.8 11.7 %add_convert_fusion.1 = bf16[1536,2304]{1,0:T(8,128)(2,1)} fusion(bf16[1536,2304]{1,0:T(8,128)(2,1)S(1)} %collective-permute-done.6, bf16[1024,1536]{1,0:T(8,128)(2,1)} %get-tuple-element.163, bf16[1024,2304]{1,0:T(8,128)(2,1)S(1)} %bitcast.216), kind=kOutput, calls=%fused_computation.1 | convolution fusion | flops 7265452032 | bytes 22020096 | tf_op jit(solution)/shard_map/rd,rf->df/dot_general | solution.py:27
  604.5 5.7 fusion.3
  610.3 101.7 %shard_map.200 = (bf16[1024,1536]{1,0:T(8,128)(2,1)}, bf16[1024,640]{1,0:T(8,128)(2,1)}, f32[8,1536]{1,0:T(8,128)}, bf16[512,1536]{1,0:T(8,128)(2,1)}, bf16[512,...) custom-call(f32[1,1536]{1,0:T(1,128)} %get-tuple-element.313.refs_3_.refs_0_, bf16[4,192,1408]{2,1,0:T(8,128)(2,1)} %bitcast.185, ...), custom_call_target="tpu_custom_call" | custom-call | flops 1048576 | bytes 1048576 | tf_op jit(solution)/shard_map/pallas_call | solution.py:965
  711.9 92.3 %shard_map.201 = (bf16[1024,2304]{1,0:T(8,128)(2,1)}, bf16[1024,2304]{1,0:T(8,128)(2,1)}, bf16[512,1536]{1,0:T(8,128)(2,1)}, bf16[512,1536]{1,0:T(8,128)(2,1)}, ...) custom-call(bf16[1024,1536]{1,0:T(8,128)(2,1)} %get-tuple-element.175.refs_0_, ...), custom_call_target="tpu_custom_call" | custom-call | flops 1048576 | bytes 1048576 | tf_op jit(solution)/shard_map/pallas_call | solution.py:586
  804.3 11.7 %convolution_convert_fusion.1 = bf16[1536,2304]{1,0:T(8,128)(2,1)} fusion(bf16[1024,1536]{1,0:T(8,128)(2,1)S(1)} %copy-done.36, bf16[1024,2304]{1,0:T(8,128)(2,1)} %get-tuple-element.187), kind=kOutput, calls=%fused_computation.3 | convolution fusion | flops 7251296256 | bytes 14942208 | tf_op jit(solution)/shard_map/rd,rf->df/dot_general | solution.py:27
  817.9 10.3 convolution_convert_fusion
  828.5 3.3 copy-done.12
  832.6 12.7 %add_convert_fusion = bf16[1536,2304]{1,0:T(8,128)(2,1)} fusion(bf16[1536,2304]{1,0:T(8,128)(2,1)} %collective-permute-done.8, bf16[1024,1536]{1,0:T(8,128)(2,1)S(1)} %copy-done.37, bf16[1024,2304]{1,0:T(8,128)(2,1)} %get-tuple-element.186), kind=kOutput, calls=%fused_computation | convolution fusion | flops 7265452032 | bytes 22020096 | tf_op jit(solution)/shard_map/rd,rf->df/dot_general | solution.py:27
  845.3 5.7 fusion.2
  855.9 3.6 convolution_convert_fusion.8
  864.4 6.5 collective-permute-start.14
  870.9 108.3 %shard_map.202 = (bf16[1024,1536]{1,0:T(8,128)(2,1)}, bf16[1024,640]{1,0:T(8,128)(2,1)}, f32[8,1536]{1,0:T(8,128)}, bf16[512,1536]{1,0:T(8,128)(2,1)}, bf16[512,...) custom-call(f32[1,1536]{1,0:T(1,128)} %get-tuple-element.315.refs_3_.refs_0_, bf16[4,192,1408]{2,1,0:T(8,128)(2,1)} %bitcast.181, ...), custom_call_target="tpu_custom_call" | custom-call | flops 1048576 | bytes 1048576 | tf_op jit(solution)/shard_map/pallas_call | solution.py:965
  981.0 4.4 convolution_convert_fusion.9
  994.2 4.5 collective-permute-start.11
  998.8 3.0 collective-permute-start.12
  1005.5 3.0 collective-permute-done.12
  1008.5 7.2 select_convert_fusion
  1015.7 5.7 copy.211
  1024.7 54.1 %shard_map.203 = (bf16[1024,1536]{1,0:T(8,128)(2,1)}, f32[8,1536]{1,0:T(8,128)}) custom-call(bf16[512,1536]{1,0:T(8,128)(2,1)} %get-tuple-element.210.part, bf16[512,1536]{1,0:T(8,128)(2,1)} %get-tuple-element.211.sum_a, bf16[1024,1536]{1,0:T(8,128)(2,1)} %get-tuple-element.207.grad, bf16[1024,1536]{1,0:T(8,128)(2,1)} %bitcast.162, ...), custom_call_target="tpu_custom_call" | custom-call | flops 1048576 | bytes 1048576 | tf_op jit(solution)/shard_map/pallas_call | solution.py:618
  1086.3 2.8 collective-permute-done.20
  1090.6 3.2 pad_maximum_fusion
  1100.5 3.2 pad_maximum_fusion.1
  1109.0 2.5 convert_element_type.214
  1117.4 3.3 collective-permute-done.16
  1126.3 7.5 collective-permute-done.17
  1140.2 2.9 copy.209
  1145.4 3.4 fusion.7
  1148.8 7.9 copy.208
  (275 shorter events, 98.1 us)
Async XLA Ops:
  7.2 10.0 copy-start.33
  7.2 56.9 %all-gather.15.cloned.1.call-start = ((), (), s32[]{:S(2)}) async-start(), calls=%async_computation.11 | async-start | bytes 2703360 | tf_op jit(solution)/shard_map/all_gather | solution.py:1068
  14.0 2.1 collective-permute-start
  17.8 20.9 %collective-permute-start.3 = (s32[2,512]{1,0:T(2,128)}, s32[2,512]{1,0:T(2,128)}, u32[]{:S(2)}, u32[]{:S(2)}) collective-permute-start(s32[2,512]{1,0:T(2,128)} %fusion.16), channel_id=1, source_target_pairs={{0,4},{4,0},{1,5},{5,1},{2,6},{6,2},{3,7},{7,3},{8,12},{12,8},{9,1... | collective-permute-start | bytes 12296 | tf_op jit(solution)/shard_map/ppermute | solution.py:1004
  26.5 16.2 %collective-permute-start.1 = (bf16[384,2304]{1,0:T(8,128)(2,1)}, bf16[384,2304]{1,0:T(8,128)(2,1)}, u32[]{:S(2)}, u32[]{:S(2)}) collective-permute-start(bf16[384,2304]{1,0:T(8,128)(2,1)} %bitcast.10), channel_id=1, source_target_pairs={{0,16},{16,0},{1,17},{17,1},{2,18},{18,2},{3,19},{19,3},{4,20},{20... | collective-permute-start | bytes 5308424 | tf_op jit(solution)/shard_map/ppermute | solution.py:31
  27.7 163.0 %all-gather.17.cloned.1.call-start = ((), (), s32[]{:S(2)}) async-start(), calls=%async_computation.12 | async-start | bytes 4423680 | tf_op jit(solution)/shard_map/all_gather | solution.py:1092
  28.7 11.3 collective-permute-start.2
  64.1 139.0 %all-gather.11.cloned.1.call-start = ((), (), s32[]{:S(2)}) async-start(), calls=%async_computation.5 | async-start | bytes 8847360 | tf_op jit(solution)/shard_map/all_gather | solution.py:1091
  64.9 214.7 %all-gather.19.cloned.1.call-start = ((), (), s32[]{:S(2)}) async-start(), calls=%async_computation.13 | async-start | bytes 2703360 | tf_op jit(solution)/shard_map/all_gather | solution.py:1121
  64.9 4.5 collective-permute-start.4
  203.2 185.0 %all-gather.21.cloned.1.call-start = ((), (), s32[]{:S(2)}) async-start(), calls=%async_computation.14 | async-start | bytes 4423680 | tf_op jit(solution)/shard_map/all_gather | solution.py:1123
  203.7 184.4 %all-gather.13.cloned.1.call-start = ((), (), s32[]{:S(2)}) async-start(), calls=%async_computation.6 | async-start | bytes 8847360 | tf_op jit(solution)/shard_map/all_gather | solution.py:1122
  204.3 646.6 %reduce-scatter.8.cloned.1.call-start = ((), (), s32[]{:S(2)}) async-start(), calls=%async_computation.7 | async-start | bytes 8847360 | tf_op jit(solution)/shard_map/reduce_scatter | solution.py:1181
  279.6 4.5 collective-permute-start.5
  478.3 90.2 %copy-start.39 = (bf16[1024,1536]{1,0:T(8,128)(2,1)S(1)}, bf16[1024,1536]{1,0:T(8,128)(2,1)}, u32[]{:S(2)}) copy-start(bf16[1024,1536]{1,0:T(8,128)(2,1)} %get-tuple-element.163) | copy-start | bytes 9437188
  568.5 10.6 copy-start.1
  568.5 24.3 %slice-start = ((s8[4718592]{0:T(1024)(128)(4,1)}), s8[4194304]{0:T(1024)(128)(4,1)S(1)}, s32[]{:S(2)}) async-start(s8[4718592]{0:T(1024)(128)(4,1)} %bitcast.215), calls=%async_computation.16 | async-start | bytes 8388608
  579.0 13.8 %collective-permute-start.6 = (bf16[1536,2304]{1,0:T(8,128)(2,1)S(1)}, bf16[1536,2304]{1,0:T(8,128)(2,1)S(1)}, u32[]{:S(2)}, u32[]{:S(2)}) collective-permute-start(bf16[1536,2304]{1,0:T(8,128)(2,1)S(1)} %convolution_convert_fusion.4), channel_id=1, source_target_pairs={{0,16},{16,0},{1,17},{17,1},{2,18},{18,2},{3,19},{19,3},{4,20},{20... | collective-permute-start | bytes 21233672 | tf_op jit(solution)/shard_map/ppermute | solution.py:31
  579.1 13.8 %slice-start.1 = ((s8[4718592]{0:T(1024)(128)(4,1)}), s8[524288]{0:T(1024)(128)(4,1)S(1)}, s32[]{:S(2)}) async-start(s8[4718592]{0:T(1024)(128)(4,1)} %bitcast.215), calls=%async_computation.17 | async-start | bytes 1048576
  592.4 12.1 %collective-permute-start.7 = (bf16[4,192,2304]{2,1,0:T(8,128)(2,1)S(1)}, bf16[4,192,2304]{2,1,0:T(8,128)(2,1)}, u32[]{:S(2)}, u32[]{:S(2)}) collective-permute-start(bf16[4,192,2304]{2,1,0:T(8,128)(2,1)S(1)} %dynamic-slice_bitcast_fusion.1), channel_id=1, source_target_pairs={{0,16},{16,0},{1,17},{17,1},{2,18},{18,2},{3,19},{19,3},{4,20},{20... | collective-permute-start | bytes 10616840 | tf_op jit(solution)/shard_map/ppermute | solution.py:31
  610.2 398.3 %reduce-scatter.10.cloned.1.call-start = ((), (), s32[]{:S(2)}) async-start(), calls=%async_computation.8 | async-start | bytes 4423680 | tf_op jit(solution)/shard_map/reduce_scatter | solution.py:1182
  711.9 92.4 %copy-start.36 = (bf16[1024,1536]{1,0:T(8,128)(2,1)S(1)}, bf16[1024,1536]{1,0:T(8,128)(2,1)}, u32[]{:S(2)}) copy-start(bf16[1024,1536]{1,0:T(8,128)(2,1)} %get-tuple-element.185) | copy-start | bytes 9437188
  816.0 15.8 %collective-permute-start.8 = (bf16[1536,2304]{1,0:T(8,128)(2,1)}, bf16[1536,2304]{1,0:T(8,128)(2,1)}, u32[]{:S(2)}, u32[]{:S(2)}) collective-permute-start(bf16[1536,2304]{1,0:T(8,128)(2,1)} %convolution_convert_fusion.1), channel_id=1, source_target_pairs={{0,16},{16,0},{1,17},{17,1},{2,18},{18,2},{3,19},{19,3},{4,20},{20... | collective-permute-start | bytes 21233672 | tf_op jit(solution)/shard_map/ppermute | solution.py:31
  816.1 199.6 %reduce-scatter.14.cloned.1.call-start = ((), (), s32[]{:S(2)}) async-start(), calls=%async_computation.10 | async-start | bytes 4423680 | tf_op jit(solution)/shard_map/reduce_scatter | solution.py:1182
  831.8 13.5 %collective-permute-start.9 = (bf16[4,192,2304]{2,1,0:T(8,128)(2,1)S(1)}, bf16[4,192,2304]{2,1,0:T(8,128)(2,1)}, u32[]{:S(2)}, u32[]{:S(2)}) collective-permute-start(bf16[4,192,2304]{2,1,0:T(8,128)(2,1)S(1)} %dynamic-slice_bitcast_fusion), channel_id=1, source_target_pairs={{0,16},{16,0},{1,17},{17,1},{2,18},{18,2},{3,19},{19,3},{4,20},{20... | collective-permute-start | bytes 10616840 | tf_op jit(solution)/shard_map/ppermute | solution.py:31
  851.0 164.7 %reduce-scatter.12.cloned.1.call-start = ((), (), s32[]{:S(2)}) async-start(), calls=%async_computation.9 | async-start | bytes 8847360 | tf_op jit(solution)/shard_map/reduce_scatter | solution.py:1181
  851.6 252.1 %reduce-scatter.16.cloned.1.call-start = ((), (), s32[]{:S(2)}) async-start(), calls=%async_computation.15 | async-start | bytes 4423680
  852.9 148.9 %collective-permute-start.10 = (bf16[1024,1536]{1,0:T(8,128)(2,1)S(1)}, bf16[1024,1536]{1,0:T(8,128)(2,1)}, u32[]{:S(2)}, u32[]{:S(2)}) collective-permute-start(bf16[1024,1536]{1,0:T(8,128)(2,1)S(1)} %copy-done), channel_id=1, source_target_pairs={{16,0},{17,1},{18,2},{19,3},{20,4},{21,5},{22,6},{23,7},{24,8},{25... | collective-permute-start | bytes 9437192 | tf_op jit(solution)/shard_map/ppermute | solution.py:1151
  864.4 144.1 %collective-permute-start.14 = (bf16[1536,1152]{0,1:T(8,128)(2,1)}, bf16[1536,1152]{0,1:T(8,128)(2,1)}, u32[]{:S(2)}, u32[]{:S(2)}) collective-permute-start(bf16[1536,1152]{0,1:T(8,128)(2,1)} %fusion.5), channel_id=1, source_target_pairs={{0,16},{1,17},{2,18},{3,19},{4,20},{5,21},{6,22},{7,23},{8,24},{9,... | collective-permute-start | bytes 10616840 | tf_op jit(solution)/shard_map/ppermute | solution.py:1202
  988.0 4.9 copy-start.26
  990.7 17.7 %collective-permute-start.13 = (bf16[1536,1152]{0,1:T(8,128)(2,1)}, bf16[1536,1152]{0,1:T(8,128)(2,1)}, u32[]{:S(2)}, u32[]{:S(2)}) collective-permute-start(bf16[1536,1152]{0,1:T(8,128)(2,1)} %fusion.4), channel_id=1, source_target_pairs={{16,0},{17,1},{18,2},{19,3},{20,4},{21,5},{22,6},{23,7},{24,8},{25... | collective-permute-start | bytes 10616840 | tf_op jit(solution)/shard_map/ppermute | solution.py:1201
  992.9 5.9 copy-start.6
  994.2 7.6 copy-start.3
  994.2 9.6 collective-permute-start.11
  998.8 9.7 collective-permute-start.12
  1022.4 64.0 %collective-permute-start.21 = (f32[2,1536]{1,0:T(2,128)S(1)}, f32[2,1536]{1,0:T(2,128)S(1)}, u32[]{:S(2)}, u32[]{:S(2)}) collective-permute-start(f32[2,1536]{1,0:T(2,128)S(1)} %pad_maximum_fusion.10), channel_id=1, source_target_pairs={{0,16},{1,17},{2,18},{3,19},{4,20},{5,21},{6,22},{7,23},{8,24},{9,... | collective-permute-start | bytes 36872 | tf_op jit(solution)/shard_map/ppermute | solution.py:1214
  1078.8 19.4 %collective-permute-start.15 = (bf16[1024,1536]{1,0:T(8,128)(2,1)}, bf16[1024,1536]{1,0:T(8,128)(2,1)}, u32[]{:S(2)}, u32[]{:S(2)}) collective-permute-start(bf16[1024,1536]{1,0:T(8,128)(2,1)} %get-tuple-element.212), channel_id=1, source_target_pairs={{16,0},{17,1},{18,2},{19,3},{20,4},{21,5},{22,6},{23,7},{24,8},{25... | collective-permute-start | bytes 9437192 | tf_op jit(solution)/shard_map/ppermute | solution.py:1151
  1082.3 8.3 copy-start.4
  1082.3 6.9 collective-permute-start.20
  1089.2 4.6 collective-permute-start.22
  1093.8 3.8 collective-permute-start.23
  1105.9 9.5 copy-start.14
  1105.9 9.5 copy-start.15
  1113.2 7.5 collective-permute-start.16
  1115.5 7.5 copy-start.17
  1115.5 23.2 %collective-permute-start.19 = (bf16[192,2304]{1,0:T(8,128)(2,1)}, bf16[192,2304]{1,0:T(8,128)(2,1)}, u32[]{:S(2)}, u32[]{:S(2)}) collective-permute-start(bf16[192,2304]{1,0:T(8,128)(2,1)} %broadcast_select_fusion.8), channel_id=1, source_target_pairs={{0,16},{16,0},{1,17},{17,1},{2,18},{18,2},{3,19},{19,3},{4,20},{20... | collective-permute-start | bytes 2654216 | tf_op jit(solution)/shard_map/ppermute | solution.py:31
  1116.9 26.2 %collective-permute-start.18 = (bf16[384,2304]{1,0:T(8,128)(2,1)}, bf16[384,2304]{1,0:T(8,128)(2,1)}, u32[]{:S(2)}, u32[]{:S(2)}) collective-permute-start(bf16[384,2304]{1,0:T(8,128)(2,1)} %broadcast_select_fusion.4), channel_id=1, source_target_pairs={{0,16},{16,0},{1,17},{17,1},{2,18},{18,2},{3,19},{19,3},{4,20},{20... | collective-permute-start | bytes 5308424 | tf_op jit(solution)/shard_map/ppermute | solution.py:31
  1120.7 13.1 %collective-permute-start.17 = (bf16[400,256]{0,1:T(8,128)(2,1)S(1)}, bf16[400,256]{0,1:T(8,128)(2,1)S(1)}, u32[]{:S(2)}, u32[]{:S(2)}) collective-permute-start(bf16[400,256]{0,1:T(8,128)(2,1)S(1)} %add_convert_fusion.3), channel_id=1, source_target_pairs={{0,2},{2,0},{1,3},{3,1},{4,6},{6,4},{5,7},{7,5},{8,10},{10,8},{9,1... | collective-permute-start | bytes 614408 | tf_op jit(solution)/shard_map/ppermute | solution.py:1235
  (29 other events, 94.5 us)
Sparse Core Ops, SparseCore 0:
  27.8 36.2 all-gather.14
  66.0 57.9 all-gather.16
  126.3 76.7 all-gather.10
  205.4 35.8 all-gather.18
  243.0 47.2 all-gather.20
  292.5 82.3 all-gather.12
  610.3 86.5 reduce-scatter.7
  816.2 46.7 reduce-scatter.9
  866.1 51.5 reduce-scatter.13
  920.6 84.8 reduce-scatter.11
  1021.6 45.1 reduce-scatter.15

commit v2 on v1

--- a/solution.py
+++ b/solution.py
@@ -1186,9 +1186,7 @@
         attn_grad, lin_grad, gain_two, part_b, sum_a, _ = attention_backward(upstream, sum_a, grad_b, k, weights, places)
         gain_two = jnp.sum(gain_two, axis=0)
         if layer == 0:
-            part_b, down_grads[1], out_low, out_high, in_high = lax.optimization_barrier(
-                (part_b, down_grads[1], out_low, out_high, in_high)
-            )
+            part_b, down_grads[1] = lax.optimization_barrier((part_b, down_grads[1]))
         lin_w = dot("rd,re->de", k["normed"], lin_grad)
         out_w = dot("rd,re->de", attn_grad, k["attended"])
         bias = jnp.sum(lin_grad.astype(F32), axis=0)
@@ -1209,6 +1207,7 @@
     packed_total = lax.psum_scatter(packed_total, ranks, scatter_dimension=0, tiled=True).astype(F32)
     in_grads[0], gain_one = last_grads(last_part, sum_a, attn_grad, kept[0]["layer_in"], attn_weights[0][2][:1])
     gains_grads[0] = jnp.stack([jnp.sum(gain_one, axis=0), gain_two])
+    in_grads[0], out_low, out_high, in_high = lax.optimization_barrier((in_grads[0], out_low, out_high, in_high))
     in_low = to_low(in_grads[0])
     low = lax.ppermute(gains_grads[0], "section", [(1, 0)])
     high = lax.ppermute(gains_grads[1], "section", [(0, 1)])
@@ -1230,7 +1229,6 @@
     kv_bias = bias[heads_here:].reshape(1, -1)
     kv_bias = jnp.pad(kv_bias, ((0, 15), (0, -kv_bias.shape[1] % (2 * HEAD))))
     mine = jnp.concatenate([kv_narrow.reshape(shard, 2 * HEAD), kv_bias[:, : 2 * HEAD]]).astype(BF16)
-    mine, gate_up_grads, down_grads = lax.optimization_barrier((mine, gate_up_grads, down_grads))
     mine = (mine.astype(F32) + lax.ppermute(mine, "tp", [(0, 1), (1, 0), (2, 3), (3, 2)]).astype(F32)).astype(BF16)
     theirs = lax.ppermute(mine, "tp", [(0, 2), (2, 0), (1, 3), (3, 1)])
     mine, theirs = mine.astype(F32), theirs.astype(F32)

time: 1170 us -> 1150 us (0.983)
    unnamed x105 -> x81, local copies, waits for them, and re-layouts: 39.1 us -> 32.4 us
  transfers between devices with their start and end apart: 35 -> 35, of which waited for: 11 -> 9; matrix products, arithmetic and copies ran while one was open for 14% -> 16% of each run, Pallas kernels for 56% -> 56%
where the time goes in v2:
time: 1150 us
  Pallas kernels  827 us (72%)
  matrix products  78.4 us (7%)
  other arithmetic  74.7 us (6%)
  local copies, waits for them, and re-layouts  64.3 us (6%)
  waiting for transfers between devices  51.7 us (4%)
  starting transfers between devices  34.3 us (3%)
  between operations  15 us (1%)
    pallas_call x2, Pallas kernels, attention_forward(): pl.pallas_call(functools.partial(attention_forward_kernel, low), out_shap...  218 us
    pallas_call x2, Pallas kernels, attention_backward(): pl.pallas_call(attention_backward_kernel, out_shape=outs, in_specs=[VMEM]...  208 us
    pallas_call x2, Pallas kernels, ffn_backward(): pl.pallas_call(functools.partial(ffn_backward_kernel, low), out_shape=[wi...  183 us
    pallas_call x2, Pallas kernels, ffn_forward(): pl.pallas_call(functools.partial(ffn_forward_kernel, lead), out_shape=[bo...  165 us
    dot_general x10, matrix products, dot(): return jnp.einsum(form, left, right, preferred_element_type=F32)  78.4 us
    pallas_call x1, Pallas kernels, last_grads(): pl.pallas_call(last_kernel, out_shape=[jax.ShapeDtypeStruct(grad.shape, B...  53.5 us
    unnamed x81, local copies, waits for them, and re-layouts  32.4 us
  transfers between devices with their start and end apart: 35, of which 9 were waited for; matrix products, arithmetic and copies ran while one was open for 16% of the time, Pallas kernels for 56%

profile of v2, /device:TPU:0, one launch (start us, length us, event | category | flops | bytes accessed | tf_op | source)
XLA Modules:
  0.0 1145.4 jit_solution(9321281034232633057)
XLA Ops:
  17.8 2.9 collective-permute-start.3
  20.7 3.5 pad_dynamic-slice_fusion.1
  24.2 2.3 copy.182
  29.4 2.8 negate_select_fusion
  32.3 3.8 constant_dynamic-slice_fusion.8
  36.0 2.7 copy.181
  40.1 2.7 broadcast_select_fusion.10
  42.8 3.5 bitcast_select_fusion
  46.3 17.8 %all-gather.15.cloned.1.call-done = bf16[768,1408]{1,0:T(8,128)(2,1)} async-done(((bf16[192,1408]{1,0:T(8,128)(2,1)}), bf16[768,1408]{1,0:T(8,128)(2,1)}) %all-gather.15.cloned.1.call-update) | async-done | bytes 2162704 | tf_op jit(solution)/shard_map/all_gather | solution.py:1068
  66.7 2.7 collective-permute-done.4.refs_3_.refs_2_
  73.0 117.4 %shard_map.195 = (bf16[1024,1536]{1,0:T(8,128)(2,1)}, bf16[1024,384]{1,0:T(8,128)(2,1)}, bf16[2048,256]{1,0:T(8,128)(2,1)}, f32[1024,128]{1,0:T(8,128)}, bf16[10...) custom-call(f32[1,1536]{1,0:T(1,128)} %get-tuple-element.306.refs_0_.gain, ...), custom_call_target="tpu_custom_call" | custom-call | flops 1048576 | bytes 1048576 | tf_op jit(solution)/shard_map/pallas_call | solution.py:822
  190.5 12.6 %all-gather.11.cloned.1.call-done.refs_4_ = bf16[1536,2304]{1,0:T(8,128)(2,1)} async-done(((bf16[384,2304]{1,0:T(8,128)(2,1)}), bf16[1536,2304]{1,0:T(8,128)(2,1)}) %all-gather.11.cloned.1.call-update) | async-done | bytes 7077904 | tf_op jit(solution)/shard_map/all_gather | solution.py:1091
  204.3 74.9 %shard_map.196 = (bf16[1024,1536]{1,0:T(8,128)(2,1)}, bf16[1024,2304]{1,0:T(8,128)(2,1)}, bf16[1024,2304]{1,0:T(8,128)(2,1)}, bf16[1024,2304]{1,0:T(8,128)(2,1)}...) custom-call(bf16[1024,1536]{1,0:T(8,128)(2,1)} %bitcast.159, ...), custom_call_target="tpu_custom_call" | custom-call | flops 1048576 | bytes 1048576 | tf_op jit(solution)/shard_map/pallas_call | solution.py:458
  279.5 3.8 constant_dynamic-slice_fusion.5
  287.4 100.3 %shard_map.197 = (bf16[1024,1536]{1,0:T(8,128)(2,1)}, bf16[1024,384]{1,0:T(8,128)(2,1)}, bf16[2048,256]{1,0:T(8,128)(2,1)}, f32[1024,128]{1,0:T(8,128)}, bf16[10...) custom-call(f32[1,1536]{1,0:T(1,128)} %get-tuple-element.304.refs_0_, ...), custom_call_target="tpu_custom_call" | custom-call | flops 1048576 | bytes 1048576 | tf_op jit(solution)/shard_map/pallas_call | solution.py:822
  387.8 90.2 %shard_map.198 = (bf16[1024,1536]{1,0:T(8,128)(2,1)}, bf16[1024,2304]{1,0:T(8,128)(2,1)}, bf16[1024,2304]{1,0:T(8,128)(2,1)}, bf16[1024,2304]{1,0:T(8,128)(2,1)}...) custom-call(bf16[1024,1536]{1,0:T(8,128)(2,1)} %get-tuple-element.144.refs_0_.refs_12_.refs_7_, ...), custom_call_target="tpu_custom_call" | custom-call | flops 1048576 | bytes 1048576 | tf_op jit(solution)/shard_map/pallas_call | solution.py:458
  478.0 90.3 %shard_map.199 = (bf16[1024,2304]{1,0:T(8,128)(2,1)}, bf16[1024,2304]{1,0:T(8,128)(2,1)}, bf16[512,1536]{1,0:T(8,128)(2,1)}, bf16[512,1536]{1,0:T(8,128)(2,1)}, bf16[512,1536]{1,0:T(8,128)(2,1)}) custom-call(bf16[1024,1536]{1,0:T(8,128)(2,1)} %bitcast.163, bf16[512,1536]{1,0:T(8,128)(2,1)} %get-tuple-element.160.refs_1_, ...), custom_call_target="tpu_custom_call" | custom-call | flops 1048576 | bytes 1048576 | tf_op jit(solution)/shard_map/pallas_call | solution.py:586
  568.3 10.5 convolution_convert_fusion.4
  578.9 10.4 convolution_convert_fusion.3
  589.5 2.6 copy-done.7
  592.7 11.7 %add_convert_fusion.1 = bf16[1536,2304]{1,0:T(8,128)(2,1)} fusion(bf16[1536,2304]{1,0:T(8,128)(2,1)S(1)} %collective-permute-done.6, bf16[1024,1536]{1,0:T(8,128)(2,1)} %get-tuple-element.159, bf16[1024,2304]{1,0:T(8,128)(2,1)S(1)} %bitcast.216), kind=kOutput, calls=%fused_computation.1 | convolution fusion | flops 7265452032 | bytes 22020096 | tf_op jit(solution)/shard_map/rd,rf->df/dot_general | solution.py:27
  604.4 5.7 fusion.3
  610.2 101.5 %shard_map.200 = (bf16[1024,1536]{1,0:T(8,128)(2,1)}, bf16[1024,640]{1,0:T(8,128)(2,1)}, f32[8,1536]{1,0:T(8,128)}, bf16[512,1536]{1,0:T(8,128)(2,1)}, bf16[512,...) custom-call(f32[1,1536]{1,0:T(1,128)} %get-tuple-element.305.refs_3_.refs_0_, bf16[4,192,1408]{2,1,0:T(8,128)(2,1)} %bitcast.185, ...), custom_call_target="tpu_custom_call" | custom-call | flops 1048576 | bytes 1048576 | tf_op jit(solution)/shard_map/pallas_call | solution.py:965
  711.7 92.4 %shard_map.201 = (bf16[1024,2304]{1,0:T(8,128)(2,1)}, bf16[1024,2304]{1,0:T(8,128)(2,1)}, bf16[512,1536]{1,0:T(8,128)(2,1)}, bf16[512,1536]{1,0:T(8,128)(2,1)}, ...) custom-call(bf16[1024,1536]{1,0:T(8,128)(2,1)} %get-tuple-element.171.refs_0_, ...), custom_call_target="tpu_custom_call" | custom-call | flops 1048576 | bytes 1048576 | tf_op jit(solution)/shard_map/pallas_call | solution.py:586
  804.1 11.7 %convolution_convert_fusion.1 = bf16[1536,2304]{1,0:T(8,128)(2,1)} fusion(bf16[1024,1536]{1,0:T(8,128)(2,1)S(1)} %copy-done.24, bf16[1024,2304]{1,0:T(8,128)(2,1)} %get-tuple-element.183), kind=kOutput, calls=%fused_computation.3 | convolution fusion | flops 7251296256 | bytes 14942208 | tf_op jit(solution)/shard_map/rd,rf->df/dot_general | solution.py:27
  816.1 10.6 convolution_convert_fusion
  827.0 3.4 copy-done.6
  831.1 12.7 %add_convert_fusion = bf16[1536,2304]{1,0:T(8,128)(2,1)} fusion(bf16[1536,2304]{1,0:T(8,128)(2,1)} %collective-permute-done.8, bf16[1024,1536]{1,0:T(8,128)(2,1)S(1)} %copy-done.25, bf16[1024,2304]{1,0:T(8,128)(2,1)} %get-tuple-element.182), kind=kOutput, calls=%fused_computation | convolution fusion | flops 7265452032 | bytes 22020096 | tf_op jit(solution)/shard_map/rd,rf->df/dot_general | solution.py:27
  843.8 5.7 fusion.2
  852.5 2.7 convolution_convert_fusion.8
  860.0 4.2 collective-permute-start.11
  864.2 106.4 %shard_map.202 = (bf16[1024,1536]{1,0:T(8,128)(2,1)}, bf16[1024,640]{1,0:T(8,128)(2,1)}, f32[8,1536]{1,0:T(8,128)}, bf16[512,1536]{1,0:T(8,128)(2,1)}, bf16[512,...) custom-call(f32[1,1536]{1,0:T(1,128)} %get-tuple-element.307.refs_3_.refs_0_, bf16[4,192,1408]{2,1,0:T(8,128)(2,1)} %bitcast.181, ...), custom_call_target="tpu_custom_call" | custom-call | flops 1048576 | bytes 1048576 | tf_op jit(solution)/shard_map/pallas_call | solution.py:965
  972.4 3.5 convolution_convert_fusion.9
  983.8 4.5 add_convert_fusion.2
  988.4 8.4 collective-permute-start.13
  996.8 3.0 collective-permute-start.14
  1001.3 7.6 select_convert_fusion
  1009.0 5.8 copy.211
  1014.8 53.5 %shard_map.203 = (bf16[1024,1536]{1,0:T(8,128)(2,1)}, f32[8,1536]{1,0:T(8,128)}) custom-call(bf16[512,1536]{1,0:T(8,128)(2,1)} %get-tuple-element.202.part, bf16[512,1536]{1,0:T(8,128)(2,1)} %get-tuple-element.203.sum_a, bf16[1024,1536]{1,0:T(8,128)(2,1)} %get-tuple-element.199.grad, bf16[1024,1536]{1,0:T(8,128)(2,1)} %bitcast.162, ...), custom_call_target="tpu_custom_call" | custom-call | flops 1048576 | bytes 1048576 | tf_op jit(solution)/shard_map/pallas_call | solution.py:618
  1070.6 2.9 broadcast_select_fusion.4
  1076.3 5.1 broadcast_select_fusion.1
  1085.7 3.2 pad_maximum_fusion
  1090.0 2.9 copy.209
  1095.3 3.3 fusion.7
  1098.6 7.9 copy.208
  1112.9 5.2 pad_maximum_fusion.1
  1120.4 2.5 collective-permute-start.17
  1125.6 10.1 collective-permute-done.17
  (250 shorter events, 74.1 us)
Async XLA Ops:
  7.2 10.0 copy-start.21
  7.2 56.9 %all-gather.15.cloned.1.call-start = ((), (), s32[]{:S(2)}) async-start(), calls=%async_computation.11 | async-start | bytes 2703360 | tf_op jit(solution)/shard_map/all_gather | solution.py:1068
  14.0 2.1 collective-permute-start
  17.8 21.0 %collective-permute-start.3 = (s32[2,512]{1,0:T(2,128)}, s32[2,512]{1,0:T(2,128)}, u32[]{:S(2)}, u32[]{:S(2)}) collective-permute-start(s32[2,512]{1,0:T(2,128)} %fusion.16), channel_id=1, source_target_pairs={{0,4},{4,0},{1,5},{5,1},{2,6},{6,2},{3,7},{7,3},{8,12},{12,8},{9,1... | collective-permute-start | bytes 12296 | tf_op jit(solution)/shard_map/ppermute | solution.py:1004
  26.6 16.2 %collective-permute-start.1 = (bf16[384,2304]{1,0:T(8,128)(2,1)}, bf16[384,2304]{1,0:T(8,128)(2,1)}, u32[]{:S(2)}, u32[]{:S(2)}) collective-permute-start(bf16[384,2304]{1,0:T(8,128)(2,1)} %bitcast.10), channel_id=1, source_target_pairs={{0,16},{16,0},{1,17},{17,1},{2,18},{18,2},{3,19},{19,3},{4,20},{20... | collective-permute-start | bytes 5308424 | tf_op jit(solution)/shard_map/ppermute | solution.py:31
  27.7 162.8 %all-gather.17.cloned.1.call-start = ((), (), s32[]{:S(2)}) async-start(), calls=%async_computation.12 | async-start | bytes 4423680 | tf_op jit(solution)/shard_map/all_gather | solution.py:1092
  28.7 11.4 collective-permute-start.2
  64.1 139.0 %all-gather.11.cloned.1.call-start = ((), (), s32[]{:S(2)}) async-start(), calls=%async_computation.5 | async-start | bytes 8847360 | tf_op jit(solution)/shard_map/all_gather | solution.py:1091
  64.9 214.4 %all-gather.19.cloned.1.call-start = ((), (), s32[]{:S(2)}) async-start(), calls=%async_computation.13 | async-start | bytes 2703360 | tf_op jit(solution)/shard_map/all_gather | solution.py:1121
  64.9 4.5 collective-permute-start.4
  203.1 184.6 %all-gather.21.cloned.1.call-start = ((), (), s32[]{:S(2)}) async-start(), calls=%async_computation.14 | async-start | bytes 4423680 | tf_op jit(solution)/shard_map/all_gather | solution.py:1123
  203.7 184.1 %all-gather.13.cloned.1.call-start = ((), (), s32[]{:S(2)}) async-start(), calls=%async_computation.6 | async-start | bytes 8847360 | tf_op jit(solution)/shard_map/all_gather | solution.py:1122
  204.3 645.3 %reduce-scatter.8.cloned.1.call-start = ((), (), s32[]{:S(2)}) async-start(), calls=%async_computation.7 | async-start | bytes 8847360 | tf_op jit(solution)/shard_map/reduce_scatter | solution.py:1181
  279.3 4.5 collective-permute-start.5
  478.0 90.3 %copy-start.27 = (bf16[1024,1536]{1,0:T(8,128)(2,1)S(1)}, bf16[1024,1536]{1,0:T(8,128)(2,1)}, u32[]{:S(2)}) copy-start(bf16[1024,1536]{1,0:T(8,128)(2,1)} %get-tuple-element.159) | copy-start | bytes 9437188
  568.3 10.6 copy-start.1
  568.3 24.4 %slice-start = ((s8[4718592]{0:T(1024)(128)(4,1)}), s8[4194304]{0:T(1024)(128)(4,1)S(1)}, s32[]{:S(2)}) async-start(s8[4718592]{0:T(1024)(128)(4,1)} %bitcast.215), calls=%async_computation.16 | async-start | bytes 8388608
  578.8 13.9 %collective-permute-start.6 = (bf16[1536,2304]{1,0:T(8,128)(2,1)S(1)}, bf16[1536,2304]{1,0:T(8,128)(2,1)S(1)}, u32[]{:S(2)}, u32[]{:S(2)}) collective-permute-start(bf16[1536,2304]{1,0:T(8,128)(2,1)S(1)} %convolution_convert_fusion.4), channel_id=1, source_target_pairs={{0,16},{16,0},{1,17},{17,1},{2,18},{18,2},{3,19},{19,3},{4,20},{20... | collective-permute-start | bytes 21233672 | tf_op jit(solution)/shard_map/ppermute | solution.py:31
  578.9 13.8 %slice-start.1 = ((s8[4718592]{0:T(1024)(128)(4,1)}), s8[524288]{0:T(1024)(128)(4,1)S(1)}, s32[]{:S(2)}) async-start(s8[4718592]{0:T(1024)(128)(4,1)} %bitcast.215), calls=%async_computation.17 | async-start | bytes 1048576
  592.2 12.2 %collective-permute-start.7 = (bf16[4,192,2304]{2,1,0:T(8,128)(2,1)S(1)}, bf16[4,192,2304]{2,1,0:T(8,128)(2,1)}, u32[]{:S(2)}, u32[]{:S(2)}) collective-permute-start(bf16[4,192,2304]{2,1,0:T(8,128)(2,1)S(1)} %dynamic-slice_bitcast_fusion.1), channel_id=1, source_target_pairs={{0,16},{16,0},{1,17},{17,1},{2,18},{18,2},{3,19},{19,3},{4,20},{20... | collective-permute-start | bytes 10616840 | tf_op jit(solution)/shard_map/ppermute | solution.py:31
  610.1 389.8 %reduce-scatter.10.cloned.1.call-start = ((), (), s32[]{:S(2)}) async-start(), calls=%async_computation.8 | async-start | bytes 4423680 | tf_op jit(solution)/shard_map/reduce_scatter | solution.py:1182
  711.7 92.4 %copy-start.24 = (bf16[1024,1536]{1,0:T(8,128)(2,1)S(1)}, bf16[1024,1536]{1,0:T(8,128)(2,1)}, u32[]{:S(2)}) copy-start(bf16[1024,1536]{1,0:T(8,128)(2,1)} %get-tuple-element.181) | copy-start | bytes 9437188
  815.8 15.0 %collective-permute-start.8 = (bf16[1536,2304]{1,0:T(8,128)(2,1)}, bf16[1536,2304]{1,0:T(8,128)(2,1)}, u32[]{:S(2)}, u32[]{:S(2)}) collective-permute-start(bf16[1536,2304]{1,0:T(8,128)(2,1)} %convolution_convert_fusion.1), channel_id=1, source_target_pairs={{0,16},{16,0},{1,17},{17,1},{2,18},{18,2},{3,19},{19,3},{4,20},{20... | collective-permute-start | bytes 21233672 | tf_op jit(solution)/shard_map/ppermute | solution.py:31
  815.9 193.1 %reduce-scatter.14.cloned.1.call-start = ((), (), s32[]{:S(2)}) async-start(), calls=%async_computation.10 | async-start | bytes 4423680 | tf_op jit(solution)/shard_map/reduce_scatter | solution.py:1182
  826.7 4.4 copy-start.25
  830.4 13.4 %collective-permute-start.9 = (bf16[4,192,2304]{2,1,0:T(8,128)(2,1)S(1)}, bf16[4,192,2304]{2,1,0:T(8,128)(2,1)}, u32[]{:S(2)}, u32[]{:S(2)}) collective-permute-start(bf16[4,192,2304]{2,1,0:T(8,128)(2,1)S(1)} %dynamic-slice_bitcast_fusion), channel_id=1, source_target_pairs={{0,16},{16,0},{1,17},{17,1},{2,18},{18,2},{3,19},{19,3},{4,20},{20... | collective-permute-start | bytes 10616840 | tf_op jit(solution)/shard_map/ppermute | solution.py:31
  849.6 159.4 %reduce-scatter.12.cloned.1.call-start = ((), (), s32[]{:S(2)}) async-start(), calls=%async_computation.9 | async-start | bytes 8847360 | tf_op jit(solution)/shard_map/reduce_scatter | solution.py:1181
  850.2 258.6 %reduce-scatter.16.cloned.1.call-start = ((), (), s32[]{:S(2)}) async-start(), calls=%async_computation.15 | async-start | bytes 4423680
  860.0 140.0 %collective-permute-start.11 = (bf16[1536,1152]{0,1:T(8,128)(2,1)}, bf16[1536,1152]{0,1:T(8,128)(2,1)}, u32[]{:S(2)}, u32[]{:S(2)}) collective-permute-start(bf16[1536,1152]{0,1:T(8,128)(2,1)} %fusion.5), channel_id=1, source_target_pairs={{0,16},{1,17},{2,18},{3,19},{4,20},{5,21},{6,22},{7,23},{8,24},{9,... | collective-permute-start | bytes 10616840 | tf_op jit(solution)/shard_map/ppermute | solution.py:1200
  864.2 108.2 %copy-start.17 = (bf16[1024,384]{1,0:T(8,128)(2,1)S(1)}, bf16[1024,384]{1,0:T(8,128)(2,1)}, u32[]{:S(2)}) copy-start(bf16[1024,384]{1,0:T(8,128)(2,1)} %get-tuple-element.180.refs_16_) | copy-start | bytes 2359300
  981.1 20.2 %collective-permute-start.10 = (bf16[1536,1152]{0,1:T(8,128)(2,1)}, bf16[1536,1152]{0,1:T(8,128)(2,1)}, u32[]{:S(2)}, u32[]{:S(2)}) collective-permute-start(bf16[1536,1152]{0,1:T(8,128)(2,1)} %fusion.4), channel_id=1, source_target_pairs={{16,0},{17,1},{18,2},{19,3},{20,4},{21,5},{22,6},{23,7},{24,8},{25... | collective-permute-start | bytes 10616840 | tf_op jit(solution)/shard_map/ppermute | solution.py:1199
  982.5 91.1 %collective-permute-start.12 = (bf16[1024,1536]{1,0:T(8,128)(2,1)S(1)}, bf16[1024,1536]{1,0:T(8,128)(2,1)}, u32[]{:S(2)}, u32[]{:S(2)}) collective-permute-start(bf16[1024,1536]{1,0:T(8,128)(2,1)S(1)} %copy-done), channel_id=1, source_target_pairs={{16,0},{17,1},{18,2},{19,3},{20,4},{21,5},{22,6},{23,7},{24,8},{25... | collective-permute-start | bytes 9437192 | tf_op jit(solution)/shard_map/ppermute | solution.py:1151
  983.8 16.0 %copy-start.19 = (f32[8,1536]{1,0:T(8,128)S(1)}, f32[8,1536]{1,0:T(8,128)}, u32[]{:S(2)}) copy-start(f32[8,1536]{1,0:T(8,128)} %get-tuple-element.218) | copy-start | bytes 147460
  983.8 16.0 %copy-start.18 = (f32[8,1536]{1,0:T(8,128)S(1)}, f32[8,1536]{1,0:T(8,128)}, u32[]{:S(2)}) copy-start(f32[8,1536]{1,0:T(8,128)} %get-tuple-element.219) | copy-start | bytes 147460
  983.8 16.1 %copy-start.20 = (f32[8,1536]{1,0:T(8,128)S(1)}, f32[8,1536]{1,0:T(8,128)}, u32[]{:S(2)}) copy-start(f32[8,1536]{1,0:T(8,128)} %get-tuple-element.217) | copy-start | bytes 147460
  988.4 86.4 %collective-permute-start.13 = (bf16[1024,1536]{1,0:T(8,128)(2,1)}, bf16[1024,1536]{1,0:T(8,128)(2,1)}, u32[]{:S(2)}, u32[]{:S(2)}) collective-permute-start(bf16[1024,1536]{1,0:T(8,128)(2,1)} %add_convert_fusion.2), channel_id=1, source_target_pairs={{0,16},{1,17},{2,18},{3,19},{4,20},{5,21},{6,22},{7,23},{8,24},{9,... | collective-permute-start | bytes 9437192 | tf_op jit(solution)/shard_map/ppermute | solution.py:1154
  996.8 78.1 %collective-permute-start.14 = (bf16[1024,1536]{1,0:T(8,128)(2,1)}, bf16[1024,1536]{1,0:T(8,128)(2,1)}, u32[]{:S(2)}, u32[]{:S(2)}) collective-permute-start(bf16[1024,1536]{1,0:T(8,128)(2,1)} %get-tuple-element.176.refs_11_), channel_id=1, source_target_pairs={{0,16},{1,17},{2,18},{3,19},{4,20},{5,21},{6,22},{7,23},{8,24},{9,... | collective-permute-start | bytes 9437192 | tf_op jit(solution)/shard_map/ppermute | solution.py:1154
  1000.0 81.5 %collective-permute-start.21 = (f32[2,1536]{1,0:T(2,128)S(1)}, f32[2,1536]{1,0:T(2,128)S(1)}, u32[]{:S(2)}, u32[]{:S(2)}) collective-permute-start(f32[2,1536]{1,0:T(2,128)S(1)} %pad_maximum_fusion.10), channel_id=1, source_target_pairs={{0,16},{1,17},{2,18},{3,19},{4,20},{5,21},{6,22},{7,23},{8,24},{9,... | collective-permute-start | bytes 36872 | tf_op jit(solution)/shard_map/ppermute | solution.py:1213
  1069.1 4.4 copy-start.11
  1069.2 12.3 %collective-permute-start.20 = (f32[2,1536]{1,0:T(2,128)S(1)}, f32[2,1536]{1,0:T(2,128)S(1)}, u32[]{:S(2)}, u32[]{:S(2)}) collective-permute-start(f32[2,1536]{1,0:T(2,128)S(1)} %pad_maximum_fusion.9), channel_id=1, source_target_pairs={{16,0},{17,1},{18,2},{19,3},{20,4},{21,5},{22,6},{23,7},{24,8},{25... | collective-permute-start | bytes 36872 | tf_op jit(solution)/shard_map/ppermute | solution.py:1212
  1073.6 16.0 %collective-permute-start.19 = (bf16[192,2304]{1,0:T(8,128)(2,1)S(1)}, bf16[192,2304]{1,0:T(8,128)(2,1)S(1)}, u32[]{:S(2)}, u32[]{:S(2)}) collective-permute-start(bf16[192,2304]{1,0:T(8,128)(2,1)S(1)} %broadcast_select_fusion.8), channel_id=1, source_target_pairs={{0,16},{16,0},{1,17},{17,1},{2,18},{18,2},{3,19},{19,3},{4,20},{20... | collective-permute-start | bytes 2654216 | tf_op jit(solution)/shard_map/ppermute | solution.py:31
  1074.8 18.2 %collective-permute-start.18 = (bf16[384,2304]{1,0:T(8,128)(2,1)}, bf16[384,2304]{1,0:T(8,128)(2,1)}, u32[]{:S(2)}, u32[]{:S(2)}) collective-permute-start(bf16[384,2304]{1,0:T(8,128)(2,1)} %broadcast_select_fusion.4), channel_id=1, source_target_pairs={{0,16},{16,0},{1,17},{17,1},{2,18},{18,2},{3,19},{19,3},{4,20},{20... | collective-permute-start | bytes 5308424 | tf_op jit(solution)/shard_map/ppermute | solution.py:31
  1074.9 31.7 %collective-permute-start.15 = (bf16[1024,1536]{1,0:T(8,128)(2,1)}, bf16[1024,1536]{1,0:T(8,128)(2,1)}, u32[]{:S(2)}, u32[]{:S(2)}) collective-permute-start(bf16[1024,1536]{1,0:T(8,128)(2,1)} %get-tuple-element.209), channel_id=1, source_target_pairs={{16,0},{17,1},{18,2},{19,3},{20,4},{21,5},{22,6},{23,7},{24,8},{25... | collective-permute-start | bytes 9437192 | tf_op jit(solution)/shard_map/ppermute | solution.py:1151
  1081.5 3.8 collective-permute-start.22
  1085.3 3.8 collective-permute-start.23
  1112.9 7.5 collective-permute-start.16
  1112.9 5.3 copy-start.10
  1120.4 15.2 %collective-permute-start.17 = (bf16[400,256]{0,1:T(8,128)(2,1)S(1)}, bf16[400,256]{0,1:T(8,128)(2,1)S(1)}, u32[]{:S(2)}, u32[]{:S(2)}) collective-permute-start(bf16[400,256]{0,1:T(8,128)(2,1)S(1)} %add_convert_fusion.3), channel_id=1, source_target_pairs={{0,2},{2,0},{1,3},{3,1},{4,6},{6,4},{5,7},{7,5},{8,10},{10,8},{9,1... | collective-permute-start | bytes 614408 | tf_op jit(solution)/shard_map/ppermute | solution.py:1233
  (17 other events, 52.7 us)
Sparse Core Ops, SparseCore 0:
  27.8 36.2 all-gather.14
  66.0 57.9 all-gather.16
  126.4 76.6 all-gather.10
  205.4 35.8 all-gather.18
  242.9 47.2 all-gather.20
  292.5 82.3 all-gather.12
  610.2 86.4 reduce-scatter.7
  816.0 46.7 reduce-scatter.9
  865.9 52.7 reduce-scatter.13
  921.6 83.1 reduce-scatter.11
  1014.9 46.3 reduce-scatter.15

commit v3 on v2

--- a/solution.py
+++ b/solution.py
@@ -1153,7 +1153,10 @@
     def to_high(value):
         return lax.ppermute(value, "section", [(0, 1)])
 
-    out_low, out_high = to_low(outs[0]), to_high(outs[1])
+    def exchanged(values):
+        return swap(jnp.where(first, values[1], values[0]))
+
+    out_other = exchanged(outs)
 
     in_grads = [None, None]
     gate_up_grads, down_grads, packed_grads, gains_grads = [[None, None] for _ in range(4)]
@@ -1196,22 +1199,17 @@
         bias = jnp.pad(bias, ((0, 0), (0, HEAD - bias.shape[1])))
         packed_grads[layer] = jnp.concatenate([lin_w, out_w, bias], axis=1).astype(BF16)
 
-    low = lax.ppermute(packed_grads[0], "section", [(1, 0)])
-    high = lax.ppermute(packed_grads[1], "section", [(0, 1)])
-    packed_total = jnp.where(
-        first, packed_grads[0].astype(F32) + low.astype(F32), packed_grads[1].astype(F32) + high.astype(F32)
-    ).astype(BF16)
+    packed_total = jnp.where(first, packed_grads[0], packed_grads[1]).astype(F32)
+    packed_total = (packed_total + exchanged(packed_grads).astype(F32)).astype(BF16)
     last_part, gate_up_grads[0], down_grads[0], packed_total = lax.optimization_barrier(
         (part_b, gate_up_grads[0], down_grads[0], packed_total)
     )
     packed_total = lax.psum_scatter(packed_total, ranks, scatter_dimension=0, tiled=True).astype(F32)
     in_grads[0], gain_one = last_grads(last_part, sum_a, attn_grad, kept[0]["layer_in"], attn_weights[0][2][:1])
     gains_grads[0] = jnp.stack([jnp.sum(gain_one, axis=0), gain_two])
-    in_grads[0], out_low, out_high, in_high = lax.optimization_barrier((in_grads[0], out_low, out_high, in_high))
+    in_grads[0], out_other, in_high = lax.optimization_barrier((in_grads[0], out_other, in_high))
     in_low = to_low(in_grads[0])
-    low = lax.ppermute(gains_grads[0], "section", [(1, 0)])
-    high = lax.ppermute(gains_grads[1], "section", [(0, 1)])
-    gains_grad = jnp.where(first, gains_grads[0] + low, gains_grads[1] + high)
+    gains_grad = jnp.where(first, gains_grads[0], gains_grads[1]) + exchanged(gains_grads)
     for axis in ranks:
         if lax.axis_size(axis) == 2:
             gains_grad = gains_grad + lax.ppermute(gains_grad, axis, [(0, 1), (1, 0)])
@@ -1242,7 +1240,7 @@
         other = swap(jnp.where(first, values[1], values[0]))
         return jnp.where(first, kept_half, other), jnp.where(first, other, kept_half)
 
-    section_out = to_section(outs, out_low, out_high)
+    section_out = to_section(outs, out_other, out_other)
     input_grad = to_section(in_grads, in_low, in_high)
     gate_up_grad = jnp.stack(collect(gate_up_grads))[..., :ff].astype(F32)
     down_grad = jnp.concatenate(collect(down_grads), axis=0)[:, :ff].T.astype(F32)

time: 1150 us -> 1160 us (level)
    unnamed x81 -> x103, local copies, waits for them, and re-layouts: 32.4 us -> 36.6 us
  transfers between devices with their start and end apart: 35 -> 32, of which waited for: 9 -> 10; matrix products, arithmetic and copies ran while one was open for 16% -> 15% of each run, Pallas kernels for 56% -> 56%
where the time goes in v3:
time: 1160 us
  Pallas kernels  833 us (72%)
  matrix products  80.6 us (7%)
  other arithmetic  75.9 us (7%)
  local copies, waits for them, and re-layouts  69.2 us (6%)
  waiting for transfers between devices  59.3 us (5%)
  starting transfers between devices  22.8 us (2%)
  between operations  14.9 us (1%)
    pallas_call x2, Pallas kernels, attention_forward(): pl.pallas_call(functools.partial(attention_forward_kernel, low), out_shap...  218 us
    pallas_call x2, Pallas kernels, attention_backward(): pl.pallas_call(attention_backward_kernel, out_shape=outs, in_specs=[VMEM]...  210 us
    pallas_call x2, Pallas kernels, ffn_backward(): pl.pallas_call(functools.partial(ffn_backward_kernel, low), out_shape=[wi...  183 us
    pallas_call x2, Pallas kernels, ffn_forward(): pl.pallas_call(functools.partial(ffn_forward_kernel, lead), out_shape=[bo...  165 us
    dot_general x10, matrix products, dot(): return jnp.einsum(form, left, right, preferred_element_type=F32)  80.6 us
    pallas_call x1, Pallas kernels, last_grads(): pl.pallas_call(last_kernel, out_shape=[jax.ShapeDtypeStruct(grad.shape, B...  56.4 us
    unnamed x103, local copies, waits for them, and re-layouts  36.6 us
  transfers between devices with their start and end apart: 32, of which 10 were waited for; matrix products, arithmetic and copies ran while one was open for 15% of the time, Pallas kernels for 56%

profile of v3, /device:TPU:0, one launch (start us, length us, event | category | flops | bytes accessed | tf_op | source)
XLA Modules:
  0.0 1155.6 jit_solution(729780180075475285)
XLA Ops:
  19.0 2.9 collective-permute-start.3
  23.9 3.5 pad_dynamic-slice_fusion.1
  31.2 3.5 negate_select_fusion
  34.7 3.8 constant_dynamic-slice_fusion.8
  38.4 2.6 copy.181
  42.4 2.9 broadcast_select_fusion.12
  45.3 3.5 bitcast_select_fusion
  48.8 8.1 all-gather.15.cloned.1.call-done
  59.6 2.7 collective-permute-done.4.refs_3_.refs_2_
  65.9 118.0 %shard_map.195 = (bf16[1024,1536]{1,0:T(8,128)(2,1)}, bf16[1024,384]{1,0:T(8,128)(2,1)}, bf16[2048,256]{1,0:T(8,128)(2,1)}, f32[1024,128]{1,0:T(8,128)}, bf16[10...) custom-call(f32[1,1536]{1,0:T(1,128)} %get-tuple-element.306.refs_0_.gain, ...), custom_call_target="tpu_custom_call" | custom-call | flops 1048576 | bytes 1048576 | tf_op jit(solution)/shard_map/pallas_call | solution.py:822
  183.9 13.0 %all-gather.11.cloned.1.call-done.refs_4_ = bf16[1536,2304]{1,0:T(8,128)(2,1)} async-done(((bf16[384,2304]{1,0:T(8,128)(2,1)}), bf16[1536,2304]{1,0:T(8,128)(2,1)}) %all-gather.11.cloned.1.call-update) | async-done | bytes 7077904 | tf_op jit(solution)/shard_map/all_gather | solution.py:1091
  198.2 74.9 %shard_map.196 = (bf16[1024,1536]{1,0:T(8,128)(2,1)}, bf16[1024,2304]{1,0:T(8,128)(2,1)}, bf16[1024,2304]{1,0:T(8,128)(2,1)}, bf16[1024,2304]{1,0:T(8,128)(2,1)}...) custom-call(bf16[1024,1536]{1,0:T(8,128)(2,1)} %bitcast.159, ...), custom_call_target="tpu_custom_call" | custom-call | flops 1048576 | bytes 1048576 | tf_op jit(solution)/shard_map/pallas_call | solution.py:458
  273.3 3.8 constant_dynamic-slice_fusion.5
  281.2 100.4 %shard_map.197 = (bf16[1024,1536]{1,0:T(8,128)(2,1)}, bf16[1024,384]{1,0:T(8,128)(2,1)}, bf16[2048,256]{1,0:T(8,128)(2,1)}, f32[1024,128]{1,0:T(8,128)}, bf16[10...) custom-call(f32[1,1536]{1,0:T(1,128)} %get-tuple-element.304.refs_0_, ...), custom_call_target="tpu_custom_call" | custom-call | flops 1048576 | bytes 1048576 | tf_op jit(solution)/shard_map/pallas_call | solution.py:822
  381.7 90.2 %shard_map.198 = (bf16[1024,1536]{1,0:T(8,128)(2,1)}, bf16[1024,2304]{1,0:T(8,128)(2,1)}, bf16[1024,2304]{1,0:T(8,128)(2,1)}, bf16[1024,2304]{1,0:T(8,128)(2,1)}...) custom-call(bf16[1024,1536]{1,0:T(8,128)(2,1)} %get-tuple-element.143.refs_0_.refs_12_.refs_7_, ...), custom_call_target="tpu_custom_call" | custom-call | flops 1048576 | bytes 1048576 | tf_op jit(solution)/shard_map/pallas_call | solution.py:458
  471.9 90.2 %shard_map.199 = (bf16[1024,2304]{1,0:T(8,128)(2,1)}, bf16[1024,2304]{1,0:T(8,128)(2,1)}, bf16[512,1536]{1,0:T(8,128)(2,1)}, bf16[512,1536]{1,0:T(8,128)(2,1)}, bf16[512,1536]{1,0:T(8,128)(2,1)}) custom-call(bf16[1024,1536]{1,0:T(8,128)(2,1)} %bitcast.163, bf16[512,1536]{1,0:T(8,128)(2,1)} %get-tuple-element.159.refs_1_, ...), custom_call_target="tpu_custom_call" | custom-call | flops 1048576 | bytes 1048576 | tf_op jit(solution)/shard_map/pallas_call | solution.py:586
  562.1 10.5 convolution_convert_fusion.4
  572.7 10.4 convolution_convert_fusion.3
  583.3 2.6 copy-done.12
  586.5 11.6 %add_convert_fusion.1 = bf16[1536,2304]{1,0:T(8,128)(2,1)} fusion(bf16[1536,2304]{1,0:T(8,128)(2,1)S(1)} %collective-permute-done.6, bf16[1024,1536]{1,0:T(8,128)(2,1)} %get-tuple-element.158, bf16[1024,2304]{1,0:T(8,128)(2,1)S(1)} %bitcast.217), kind=kOutput, calls=%fused_computation.1 | convolution fusion | flops 7265452032 | bytes 22020096 | tf_op jit(solution)/shard_map/rd,rf->df/dot_general | solution.py:27
  598.0 5.7 fusion.3
  603.8 101.6 %shard_map.200 = (bf16[1024,1536]{1,0:T(8,128)(2,1)}, bf16[1024,640]{1,0:T(8,128)(2,1)}, f32[8,1536]{1,0:T(8,128)}, bf16[512,1536]{1,0:T(8,128)(2,1)}, bf16[512,...) custom-call(f32[1,1536]{1,0:T(1,128)} %get-tuple-element.305.refs_3_.refs_0_, bf16[4,192,1408]{2,1,0:T(8,128)(2,1)} %bitcast.185, ...), custom_call_target="tpu_custom_call" | custom-call | flops 1048576 | bytes 1048576 | tf_op jit(solution)/shard_map/pallas_call | solution.py:965
  705.4 92.3 %shard_map.201 = (bf16[1024,2304]{1,0:T(8,128)(2,1)}, bf16[1024,2304]{1,0:T(8,128)(2,1)}, bf16[512,1536]{1,0:T(8,128)(2,1)}, bf16[512,1536]{1,0:T(8,128)(2,1)}, ...) custom-call(bf16[1024,1536]{1,0:T(8,128)(2,1)} %get-tuple-element.170.refs_0_, ...), custom_call_target="tpu_custom_call" | custom-call | flops 1048576 | bytes 1048576 | tf_op jit(solution)/shard_map/pallas_call | solution.py:586
  797.8 11.7 %convolution_convert_fusion.1 = bf16[1536,2304]{1,0:T(8,128)(2,1)} fusion(bf16[1024,1536]{1,0:T(8,128)(2,1)S(1)} %copy-done.35, bf16[1024,2304]{1,0:T(8,128)(2,1)} %get-tuple-element.182), kind=kOutput, calls=%fused_computation.3 | convolution fusion | flops 7251296256 | bytes 14942208 | tf_op jit(solution)/shard_map/rd,rf->df/dot_general | solution.py:27
  809.7 10.6 convolution_convert_fusion
  820.6 3.4 copy-done.11
  824.8 12.7 %add_convert_fusion = bf16[1536,2304]{1,0:T(8,128)(2,1)} fusion(bf16[1536,2304]{1,0:T(8,128)(2,1)} %collective-permute-done.8, bf16[1024,1536]{1,0:T(8,128)(2,1)S(1)} %copy-done.36, bf16[1024,2304]{1,0:T(8,128)(2,1)} %get-tuple-element.181), kind=kOutput, calls=%fused_computation | convolution fusion | flops 7265452032 | bytes 22020096 | tf_op jit(solution)/shard_map/rd,rf->df/dot_general | solution.py:27
  837.5 5.7 fusion.2
  846.2 3.7 convolution_convert_fusion.8
  849.9 3.6 convolution_convert_fusion.6
  853.5 108.8 %shard_map.202 = (bf16[1024,1536]{1,0:T(8,128)(2,1)}, bf16[1024,640]{1,0:T(8,128)(2,1)}, f32[8,1536]{1,0:T(8,128)}, bf16[512,1536]{1,0:T(8,128)(2,1)}, bf16[512,...) custom-call(f32[1,1536]{1,0:T(1,128)} %get-tuple-element.307.refs_3_.refs_0_, bf16[4,192,1408]{2,1,0:T(8,128)(2,1)} %bitcast.181, ...), custom_call_target="tpu_custom_call" | custom-call | flops 1048576 | bytes 1048576 | tf_op jit(solution)/shard_map/pallas_call | solution.py:965
  964.1 3.5 convolution_convert_fusion.9
  975.7 2.7 broadcast_select_fusion.5
  978.4 4.0 collective-permute-start.12
  982.6 5.9 add_convert_fusion.2
  988.5 11.1 reduce-scatter.12.cloned.1.call-done
  999.6 56.4 %shard_map.203 = (bf16[1024,1536]{1,0:T(8,128)(2,1)}, f32[8,1536]{1,0:T(8,128)}) custom-call(bf16[512,1536]{1,0:T(8,128)(2,1)} %get-tuple-element.201.part, bf16[512,1536]{1,0:T(8,128)(2,1)} %get-tuple-element.202.sum_a, bf16[1024,1536]{1,0:T(8,128)(2,1)} %get-tuple-element.198.grad, bf16[1024,1536]{1,0:T(8,128)(2,1)} %bitcast.162, ...), custom_call_target="tpu_custom_call" | custom-call | flops 1048576 | bytes 1048576 | tf_op jit(solution)/shard_map/pallas_call | solution.py:618
  1056.0 6.3 broadcast_select_fusion.4
  1064.0 5.8 copy.211
  1073.8 4.9 collective-permute-start.17
  1084.1 3.2 pad_maximum_fusion
  1088.4 2.9 copy.209
  1093.7 3.4 fusion.7
  1097.0 8.0 copy.208
  1105.0 4.1 broadcast_select_fusion.1
  1109.1 8.9 reduce-scatter.16.cloned.1.call-done
  1124.2 5.2 pad_maximum_fusion.1
  1136.5 9.4 collective-permute-done.15
  (264 shorter events, 75.9 us)
Async XLA Ops:
  7.2 49.8 %all-gather.15.cloned.1.call-start = ((), (), s32[]{:S(2)}) async-start(), calls=%async_computation.11 | async-start | bytes 2703360 | tf_op jit(solution)/shard_map/all_gather | solution.py:1068
  9.7 8.7 copy-start.32
  10.9 11.0 copy-start.24
  14.9 2.2 collective-permute-start
  18.3 165.6 %all-gather.17.cloned.1.call-start = ((), (), s32[]{:S(2)}) async-start(), calls=%async_computation.12 | async-start | bytes 4423680 | tf_op jit(solution)/shard_map/all_gather | solution.py:1092
  19.0 22.1 %collective-permute-start.3 = (s32[2,512]{1,0:T(2,128)}, s32[2,512]{1,0:T(2,128)}, u32[]{:S(2)}, u32[]{:S(2)}) collective-permute-start(s32[2,512]{1,0:T(2,128)} %fusion.16), channel_id=1, source_target_pairs={{0,4},{4,0},{1,5},{5,1},{2,6},{6,2},{3,7},{7,3},{8,12},{12,8},{9,1... | collective-permute-start | bytes 12296 | tf_op jit(solution)/shard_map/ppermute | solution.py:1004
  23.9 18.5 %collective-permute-start.2 = (bf16[192,2304]{1,0:T(8,128)(2,1)}, bf16[192,2304]{1,0:T(8,128)(2,1)}, u32[]{:S(2)}, u32[]{:S(2)}) collective-permute-start(bf16[192,2304]{1,0:T(8,128)(2,1)} %pad_dynamic-slice_fusion.2), channel_id=1, source_target_pairs={{0,16},{16,0},{1,17},{17,1},{2,18},{18,2},{3,19},{19,3},{4,20},{20... | collective-permute-start | bytes 2654216 | tf_op jit(solution)/shard_map/ppermute | solution.py:31
  29.8 15.5 %collective-permute-start.1 = (bf16[384,2304]{1,0:T(8,128)(2,1)}, bf16[384,2304]{1,0:T(8,128)(2,1)}, u32[]{:S(2)}, u32[]{:S(2)}) collective-permute-start(bf16[384,2304]{1,0:T(8,128)(2,1)} %bitcast.196), channel_id=1, source_target_pairs={{0,16},{16,0},{1,17},{17,1},{2,18},{18,2},{3,19},{19,3},{4,20},{20... | collective-permute-start | bytes 5308424 | tf_op jit(solution)/shard_map/ppermute | solution.py:31
  57.0 139.9 %all-gather.11.cloned.1.call-start = ((), (), s32[]{:S(2)}) async-start(), calls=%async_computation.5 | async-start | bytes 8847360 | tf_op jit(solution)/shard_map/all_gather | solution.py:1091
  57.7 215.4 %all-gather.19.cloned.1.call-start = ((), (), s32[]{:S(2)}) async-start(), calls=%async_computation.13 | async-start | bytes 2703360 | tf_op jit(solution)/shard_map/all_gather | solution.py:1121
  57.8 4.5 collective-permute-start.4
  196.9 184.7 %all-gather.21.cloned.1.call-start = ((), (), s32[]{:S(2)}) async-start(), calls=%async_computation.14 | async-start | bytes 4423680 | tf_op jit(solution)/shard_map/all_gather | solution.py:1123
  197.5 184.2 %all-gather.13.cloned.1.call-start = ((), (), s32[]{:S(2)}) async-start(), calls=%async_computation.6 | async-start | bytes 8847360 | tf_op jit(solution)/shard_map/all_gather | solution.py:1122
  198.1 645.1 %reduce-scatter.8.cloned.1.call-start = ((), (), s32[]{:S(2)}) async-start(), calls=%async_computation.7 | async-start | bytes 8847360 | tf_op jit(solution)/shard_map/reduce_scatter | solution.py:1184
  273.1 4.5 collective-permute-start.5
  471.9 90.2 %copy-start.38 = (bf16[1024,1536]{1,0:T(8,128)(2,1)S(1)}, bf16[1024,1536]{1,0:T(8,128)(2,1)}, u32[]{:S(2)}) copy-start(bf16[1024,1536]{1,0:T(8,128)(2,1)} %get-tuple-element.158) | copy-start | bytes 9437188
  562.1 10.6 copy-start.1
  562.1 24.3 %slice-start = ((s8[4718592]{0:T(1024)(128)(4,1)}), s8[4194304]{0:T(1024)(128)(4,1)S(1)}, s32[]{:S(2)}) async-start(s8[4718592]{0:T(1024)(128)(4,1)} %bitcast.216), calls=%async_computation.16 | async-start | bytes 8388608
  572.6 13.8 %collective-permute-start.6 = (bf16[1536,2304]{1,0:T(8,128)(2,1)S(1)}, bf16[1536,2304]{1,0:T(8,128)(2,1)S(1)}, u32[]{:S(2)}, u32[]{:S(2)}) collective-permute-start(bf16[1536,2304]{1,0:T(8,128)(2,1)S(1)} %convolution_convert_fusion.4), channel_id=1, source_target_pairs={{0,16},{16,0},{1,17},{17,1},{2,18},{18,2},{3,19},{19,3},{4,20},{20... | collective-permute-start | bytes 21233672 | tf_op jit(solution)/shard_map/ppermute | solution.py:31
  572.7 13.8 %slice-start.1 = ((s8[4718592]{0:T(1024)(128)(4,1)}), s8[524288]{0:T(1024)(128)(4,1)S(1)}, s32[]{:S(2)}) async-start(s8[4718592]{0:T(1024)(128)(4,1)} %bitcast.216), calls=%async_computation.17 | async-start | bytes 1048576
  586.0 12.1 %collective-permute-start.7 = (bf16[4,192,2304]{2,1,0:T(8,128)(2,1)S(1)}, bf16[4,192,2304]{2,1,0:T(8,128)(2,1)}, u32[]{:S(2)}, u32[]{:S(2)}) collective-permute-start(bf16[4,192,2304]{2,1,0:T(8,128)(2,1)S(1)} %dynamic-slice_bitcast_fusion.1), channel_id=1, source_target_pairs={{0,16},{16,0},{1,17},{17,1},{2,18},{18,2},{3,19},{19,3},{4,20},{20... | collective-permute-start | bytes 10616840 | tf_op jit(solution)/shard_map/ppermute | solution.py:31
  603.7 378.8 %reduce-scatter.10.cloned.1.call-start = ((), (), s32[]{:S(2)}) async-start(), calls=%async_computation.8 | async-start | bytes 4423680 | tf_op jit(solution)/shard_map/reduce_scatter | solution.py:1185
  705.4 92.4 %copy-start.35 = (bf16[1024,1536]{1,0:T(8,128)(2,1)S(1)}, bf16[1024,1536]{1,0:T(8,128)(2,1)}, u32[]{:S(2)}) copy-start(bf16[1024,1536]{1,0:T(8,128)(2,1)} %get-tuple-element.180) | copy-start | bytes 9437188
  809.5 15.0 %collective-permute-start.8 = (bf16[1536,2304]{1,0:T(8,128)(2,1)}, bf16[1536,2304]{1,0:T(8,128)(2,1)}, u32[]{:S(2)}, u32[]{:S(2)}) collective-permute-start(bf16[1536,2304]{1,0:T(8,128)(2,1)} %convolution_convert_fusion.1), channel_id=1, source_target_pairs={{0,16},{16,0},{1,17},{17,1},{2,18},{18,2},{3,19},{19,3},{4,20},{20... | collective-permute-start | bytes 21233672 | tf_op jit(solution)/shard_map/ppermute | solution.py:31
  809.5 179.0 %reduce-scatter.14.cloned.1.call-start = ((), (), s32[]{:S(2)}) async-start(), calls=%async_computation.10 | async-start | bytes 4423680 | tf_op jit(solution)/shard_map/reduce_scatter | solution.py:1185
  824.0 13.5 %collective-permute-start.9 = (bf16[4,192,2304]{2,1,0:T(8,128)(2,1)S(1)}, bf16[4,192,2304]{2,1,0:T(8,128)(2,1)}, u32[]{:S(2)}, u32[]{:S(2)}) collective-permute-start(bf16[4,192,2304]{2,1,0:T(8,128)(2,1)S(1)} %dynamic-slice_bitcast_fusion), channel_id=1, source_target_pairs={{0,16},{16,0},{1,17},{17,1},{2,18},{18,2},{3,19},{19,3},{4,20},{20... | collective-permute-start | bytes 10616840 | tf_op jit(solution)/shard_map/ppermute | solution.py:31
  843.3 156.3 %reduce-scatter.12.cloned.1.call-start = ((), (), s32[]{:S(2)}) async-start(), calls=%async_computation.9 | async-start | bytes 8847360 | tf_op jit(solution)/shard_map/reduce_scatter | solution.py:1184
  843.9 274.1 %reduce-scatter.16.cloned.1.call-start = ((), (), s32[]{:S(2)}) async-start(), calls=%async_computation.15 | async-start | bytes 4423680
  853.5 110.6 %copy-start.27 = (bf16[1024,384]{1,0:T(8,128)(2,1)S(1)}, bf16[1024,384]{1,0:T(8,128)(2,1)}, u32[]{:S(2)}) copy-start(bf16[1024,384]{1,0:T(8,128)(2,1)} %get-tuple-element.179.refs_16_) | copy-start | bytes 2359300
  972.8 9.8 collective-permute-start.10
  975.7 6.7 copy-start.29
  975.7 6.7 copy-start.28
  975.7 6.8 copy-start.30
  978.4 77.6 %collective-permute-start.11 = (bf16[1024,1536]{1,0:T(8,128)(2,1)}, bf16[1024,1536]{1,0:T(8,128)(2,1)}, u32[]{:S(2)}, u32[]{:S(2)}) collective-permute-start(bf16[1024,1536]{1,0:T(8,128)(2,1)} %broadcast_select_fusion.5), channel_id=1, source_target_pairs={{0,16},{16,0},{1,17},{17,1},{2,18},{18,2},{3,19},{19,3},{4,20},{20... | collective-permute-start | bytes 9437192 | tf_op jit(solution)/shard_map/ppermute | solution.py:31
  978.4 77.6 %collective-permute-start.12 = (bf16[1024,1536]{1,0:T(8,128)(2,1)}, bf16[1024,1536]{1,0:T(8,128)(2,1)}, u32[]{:S(2)}, u32[]{:S(2)}) collective-permute-start(bf16[1024,1536]{1,0:T(8,128)(2,1)} %get-tuple-element.175.refs_11_), channel_id=1, source_target_pairs={{0,16},{1,17},{2,18},{3,19},{4,20},{5,21},{6,22},{7,23},{8,24},{9,... | collective-permute-start | bytes 9437192 | tf_op jit(solution)/shard_map/ppermute | solution.py:1154
  1062.4 16.3 %collective-permute-start.18 = (f32[2,1536]{1,0:T(2,128)S(1)}, f32[2,1536]{1,0:T(2,128)S(1)}, u32[]{:S(2)}, u32[]{:S(2)}) collective-permute-start(f32[2,1536]{1,0:T(2,128)S(1)} %broadcast_select_fusion.16), channel_id=1, source_target_pairs={{0,16},{16,0},{1,17},{17,1},{2,18},{18,2},{3,19},{19,3},{4,20},{20... | collective-permute-start | bytes 36872 | tf_op jit(solution)/shard_map/ppermute | solution.py:31
  1062.5 42.5 %collective-permute-start.13 = (bf16[1024,1536]{1,0:T(8,128)(2,1)}, bf16[1024,1536]{1,0:T(8,128)(2,1)}, u32[]{:S(2)}, u32[]{:S(2)}) collective-permute-start(bf16[1024,1536]{1,0:T(8,128)(2,1)} %get-tuple-element.207), channel_id=1, source_target_pairs={{16,0},{17,1},{18,2},{19,3},{20,4},{21,5},{22,6},{23,7},{24,8},{25... | collective-permute-start | bytes 9437192 | tf_op jit(solution)/shard_map/ppermute | solution.py:1151
  1071.6 8.4 copy-start.13
  1071.6 8.4 copy-start.14
  1073.7 10.5 copy-start.6
  1073.8 10.4 copy-start.5
  1073.8 14.2 %collective-permute-start.17 = (bf16[192,2304]{1,0:T(8,128)(2,1)S(1)}, bf16[192,2304]{1,0:T(8,128)(2,1)S(1)}, u32[]{:S(2)}, u32[]{:S(2)}) collective-permute-start(bf16[192,2304]{1,0:T(8,128)(2,1)S(1)} %broadcast_select_fusion.10), channel_id=1, source_target_pairs={{0,16},{16,0},{1,17},{17,1},{2,18},{18,2},{3,19},{19,3},{4,20},{20... | collective-permute-start | bytes 2654216 | tf_op jit(solution)/shard_map/ppermute | solution.py:31
  1078.7 4.0 collective-permute-start.19
  1081.4 9.9 collective-permute-start.16
  1082.8 4.6 collective-permute-start.20
  1105.0 19.2 %copy-start.4 = (bf16[1024,1536]{1,0:T(8,128)(2,1)S(1)}, bf16[1024,1536]{1,0:T(8,128)(2,1)}, u32[]{:S(2)}) copy-start(bf16[1024,1536]{1,0:T(8,128)(2,1)} %broadcast_select_fusion.2) | copy-start | bytes 9437188
  1122.7 8.4 collective-permute-start.14
  1132.1 13.8 %collective-permute-start.15 = (bf16[400,256]{0,1:T(8,128)(2,1)S(1)}, bf16[400,256]{0,1:T(8,128)(2,1)S(1)}, u32[]{:S(2)}, u32[]{:S(2)}) collective-permute-start(bf16[400,256]{0,1:T(8,128)(2,1)S(1)} %add_convert_fusion.4), channel_id=1, source_target_pairs={{0,2},{2,0},{1,3},{3,1},{4,6},{6,4},{5,7},{7,5},{8,10},{10,8},{9,1... | collective-permute-start | bytes 614408 | tf_op jit(solution)/shard_map/ppermute | solution.py:1231
  (25 other events, 89.5 us)
Sparse Core Ops, SparseCore 0:
  18.4 38.4 all-gather.14
  59.4 58.3 all-gather.16
  120.2 76.6 all-gather.10
  199.2 35.8 all-gather.18
  236.8 47.2 all-gather.20
  286.3 82.3 all-gather.12
  603.9 86.4 reduce-scatter.7
  809.6 46.8 reduce-scatter.9
  860.2 52.7 reduce-scatter.13
  915.9 83.6 reduce-scatter.11
  1069.9 48.0 reduce-scatter.15
